TPU v7x, 256 devices: a whole 4x4x8 slice. The times are simulated.
256 devices in a mesh: replica: 8 (over z_lo, y), fsdp: 32 (over x, z_hi, core).
Axes of the slice: x: 4, y: 4, z: 8 (z_hi: 4, z_lo: 2; z = z_hi * 2 + z_lo), core: 2. Of those that a mesh axis runs over, the one named last changes fastest.
Arguments:
- acts: bfloat16 [8, 16384, 8192], P('replica', 'fsdp'), may hold values from -6 to 6
- doc_ids: int32 [8, 16384], P('replica', 'fsdp'), may hold values from 0 to 7, never falling along the last dimension, each value on 1 to 8192 neighbouring positions
- target: bfloat16 [8, 16384, 512], P('replica', 'fsdp'), may hold values from -6 to 6
- inner_weight: float32 [8, 8192, 512], P('replica', 'fsdp'), may hold values from -6 to 6
- adam_first: float32 [8, 8192, 512], P('replica', 'fsdp'), may hold values from -4 to 4
- adam_second: float32 [8, 8192, 512], P('replica', 'fsdp'), may hold values from 0.25 to 4
- outer_weight: float32 [8192, 512], P('fsdp'), may hold values from -6 to 6
- outer_moment: float32 [8192, 512], P('fsdp'), may hold values from -4 to 4
- fragment: int32 [1], replicated, may hold values from 0 to 3
Outputs:
- inner_out: float32 [8, 8192, 512], P('replica', 'fsdp')
- first_out: float32 [8, 8192, 512], P('replica', 'fsdp')
- second_out: float32 [8, 8192, 512], P('replica', 'fsdp')
- outer_out: float32 [8192, 512], P('fsdp')
- moment_out: float32 [8192, 512], P('fsdp')
Inputs may be any that keep to these rules, and one draw needn't show every extreme that they name: Within each group doc_ids never falls, every number of 0 to 7 occurs, each document holds at most 8192 tokens and one exactly 8192.
All inputs are finite; a program needn't handle non-finite values.
Results may differ from a plain program's by a relative error of at most 0.0033.
Values may be sent and summed in bfloat16 or wider, within the bound.
No kernel may reach another device: no remote copies, remote signals or barrier semaphores. Data moves between devices by JAX's collectives and lax.ppermute only.
A program may use at most 128 MiB of HBM per device.

v0:
```python
import math

import jax
import jax.numpy as jnp
from jax import lax
from jax.experimental import pallas as pl
from jax.experimental.pallas import tpu as pltpu
from jax.sharding import PartitionSpec as P

D = 8192
HEAD = 128
FRAGS = 4
DOCS = 8

theta_base = 500000.0
first_fix = 0.9999734386011124
second_fix = 0.9940794707796672

f32 = jnp.float32
bf16 = jnp.bfloat16
VM = pltpu.VMEM
LIMIT = 16 * 1024 * 1024
NOTE = 16
NOWHERE = 128 * 255
NT = (((1,), (1,)), ((), ()))
SCALARS = pl.BlockSpec(memory_space=pltpu.SMEM)

NX, NZ = 4, 4
TORUS = [(x, z, c) for x in range(NX) for z in range(NZ) for c in range(2)]


def place(x, z, c):
    return ((x % NX) * NZ + z % NZ) * 2 + c


def pairs(target):
    return [(place(*at), place(*target(*at))) for at in TORUS]


def way(c):
    return 1 - 2 * c


FROM_X = pairs(lambda x, z, c: (x - way(c), z, c))
FROM_Z = pairs(lambda x, z, c: (x, z - way(c), c))
TO_X = pairs(lambda x, z, c: (x + way(c), z, c))
TO_Z = pairs(lambda x, z, c: (x, z + way(c), c))
SIBLING = pairs(lambda x, z, c: (x, z, 1 - c))


def move(value, table):
    return lax.ppermute(value, "fsdp", table)


def after(value, *others):
    return lax.optimization_barrier((value,) + others)[0]


def params(limit=LIMIT):
    return pltpu.CompilerParams(vmem_limit_bytes=limit)


def cost(flops, moved):
    return pl.CostEstimate(flops=flops, bytes_accessed=moved, transcendentals=0)


def in_vmem(n):
    return [pl.BlockSpec(memory_space=VM)] * n


def turn_weight(weight, ids, first):
    rows, cols = weight.shape
    toks = ids.shape[1]

    def body(f_ref, w_ref, i_ref, o_ref):
        o_ref[:cols, :] = w_ref[...].T.astype(bf16)
        number = lax.broadcasted_iota(jnp.int32, (DOCS, toks), 0)
        token = lax.broadcasted_iota(jnp.int32, (DOCS, toks), 1) + f_ref[0]
        found = jnp.where(i_ref[...] == number, token, NOWHERE).astype(f32)
        start = jnp.min(found, axis=1, keepdims=True)
        high = jnp.floor(start * (1.0 / 128.0))
        low = start - 128.0 * high
        digits = jnp.concatenate([high, low], axis=0)
        o_ref[cols:, :] = jnp.broadcast_to(digits, (NOTE, rows)).astype(bf16)

    return pl.pallas_call(
        body,
        in_specs=[SCALARS] + in_vmem(2),
        out_specs=pl.BlockSpec(memory_space=VM),
        out_shape=jax.ShapeDtypeStruct((cols + NOTE, rows), bf16),
        compiler_params=params(),
        cost_estimate=cost(0, rows * cols * 6),
    )(first, weight, ids)


def read_notes(*values):
    rows, width = values[0].shape[-2:]
    cols = rows - NOTE

    def body(*refs):
        least = None
        for ref in refs[:-1]:
            if len(ref.shape) == 2:
                notes = [ref[cols:, :]]
            else:
                notes = [ref[i, cols:, :] for i in range(ref.shape[0])]
            for note in notes:
                digits = note.astype(f32)
                start = 128.0 * digits[:DOCS] + digits[DOCS:]
                least = start if least is None else jnp.minimum(least, start)
        refs[-1][...] = least

    return pl.pallas_call(
        body,
        in_specs=in_vmem(len(values)),
        out_specs=pl.BlockSpec(memory_space=VM),
        out_shape=jax.ShapeDtypeStruct((DOCS, width), f32),
        compiler_params=params(),
        cost_estimate=cost(0, len(values) * 100000),
    )(*values)


def token_angles(base, notes, notes_sib, ids, ids_sib, freqs):
    toks = ids.shape[1]
    half = freqs.shape[0]

    def body(b_ref, n_ref, m_ref, i_ref, j_ref, f_ref, o_ref):
        starts = jnp.minimum(n_ref[...], m_ref[...])[:, :1]
        number = lax.broadcasted_iota(jnp.int32, (DOCS, toks), 0)
        token = lax.broadcasted_iota(jnp.int32, (1, toks), 1)
        for k, ref in enumerate((i_ref, j_ref)):
            began = jnp.sum(jnp.where(ref[...] == number, starts, 0.0), axis=0, keepdims=True)
            position = (token + b_ref[k]).astype(f32) - began
            o_ref[:, k * toks : (k + 1) * toks] = f_ref[...] * position

    return pl.pallas_call(
        body,
        in_specs=[SCALARS] + in_vmem(5),
        out_specs=pl.BlockSpec(memory_space=VM),
        out_shape=jax.ShapeDtypeStruct((half, 2 * toks), f32),
        compiler_params=params(),
        cost_estimate=cost(0, half * toks * 16),
    )(base, notes, notes_sib, ids, ids_sib, freqs)


def turn_target(target, target_sib, cosine, sine):
    toks, cols = target.shape
    half = HEAD // 2

    def body(t_ref, u_ref, c_ref, s_ref, o_ref):
        for k, ref in enumerate((t_ref, u_ref)):
            here = slice(k * toks, (k + 1) * toks)
            cosv, sinv = c_ref[:, here], s_ref[:, here]
            for head in range(cols // HEAD):
                at = head * HEAD
                turned = ref[:, at : at + HEAD].astype(f32).T
                u, w = turned[:half], turned[half:]
                o_ref[at : at + half, here] = u * cosv + w * sinv
                o_ref[at + half : at + HEAD, here] = w * cosv - u * sinv

    return pl.pallas_call(
        body,
        in_specs=in_vmem(4),
        out_specs=pl.BlockSpec(memory_space=VM),
        out_shape=jax.ShapeDtypeStruct((cols, 2 * toks), f32),
        compiler_params=params(),
        cost_estimate=cost(0, toks * cols * 12),
    )(target, target_sib, cosine, sine)


PART = 4


def pick_columns(features, blocks, blocks_sib, width):
    toks, depth = features.shape
    count = blocks.shape[0]
    rows = toks // 8

    def body(b_ref, d_ref, f_ref, o_ref, *s_refs):
        for k in range(count):
            at = pl.multiple_of(d_ref[k] * width, width)
            s_refs[k // PART][k % PART] = f_ref[:, pl.ds(at, width)]
        for k in range(count):
            at = pl.multiple_of(b_ref[k] * width, width)
            o_ref[k] = f_ref[:, pl.ds(at, width)]

    def stack(n):
        return jax.ShapeDtypeStruct((n, toks, width), features.dtype)

    def spec(n):
        return pl.BlockSpec((n, rows, width), lambda i, b, d: (0, i, 0))

    parts = count // PART
    out = pl.pallas_call(
        body,
        grid_spec=pltpu.PrefetchScalarGridSpec(
            num_scalar_prefetch=2,
            grid=(toks // rows,),
            in_specs=[pl.BlockSpec((rows, depth), lambda i, b, d: (i, 0))],
            out_specs=[spec(count)] + [spec(PART)] * parts,
        ),
        out_shape=[stack(count)] + [stack(PART)] * parts,
        compiler_params=params(),
        cost_estimate=cost(0, toks * count * width * 8),
    )(blocks, blocks_sib, features)
    return out[0], out[1:]


def parts_of(pieces, far):
    used = sorted({k // PART for k in pieces})
    return [far[p] for p in used], {k: used.index(k // PART) for k in pieces}


def add_keys(pieces, own, far, weights, total):
    toks = own.shape[1]
    rows, width = weights[0].shape[-2:]
    cols = rows - NOTE
    m = len(weights)
    names = [k for held in pieces for k in held]
    n = len(names)
    held_far, part = parts_of(names, far)
    p = len(held_far)

    def body(own_ref, *refs):
        far_refs, refs = refs[:p], refs[p:]
        o_ref = refs[-1]
        values = [None, None]
        if total is not None:
            values = [refs[m][:, :toks], refs[m][:, toks:]]
        for w_ref, held in zip(refs, pieces):
            for slab, k in enumerate(held):
                w = w_ref[:cols, :] if len(w_ref.shape) == 2 else w_ref[slab, :cols, :]
                for j, block in enumerate((own_ref[k], far_refs[part[k]][k % PART])):
                    term = lax.dot_general(w, block, NT, preferred_element_type=f32)
                    values[j] = term if values[j] is None else values[j] + term
        o_ref[:, :toks] = values[0]
        o_ref[:, toks:] = values[1]

    extra = [] if total is None else [total]
    return pl.pallas_call(
        body,
        in_specs=in_vmem(1 + p + m + len(extra)),
        out_specs=pl.BlockSpec(memory_space=VM),
        out_shape=jax.ShapeDtypeStruct((cols, 2 * toks), f32),
        compiler_params=params(),
        cost_estimate=cost(4 * n * toks * cols * width, cols * toks * 8),
    )(own, *held_far, *weights, *extra)


def grads(pieces, own, far, back):
    toks, width = own.shape[1:]
    cols = back.shape[0]
    names = [k for held, _ in pieces for k in held]
    n = len(names)
    held_far, part = parts_of(names, far)
    p = len(held_far)

    def body(own_ref, *refs):
        far_refs, k_ref, refs = refs[:p], refs[p], refs[p + 1 :]
        for o_ref, (held, kind) in zip(refs, pieces):
            for slab, k in enumerate(held):
                value = jnp.dot(k_ref[:, :toks], own_ref[k], preferred_element_type=f32)
                block = far_refs[part[k]][k % PART]
                value += jnp.dot(k_ref[:, toks:], block, preferred_element_type=f32)
                o_ref[slab] = value.astype(kind)

    return pl.pallas_call(
        body,
        in_specs=in_vmem(2 + p),
        out_specs=in_vmem(len(pieces)),
        out_shape=[jax.ShapeDtypeStruct((len(held), cols, width), kind) for held, kind in pieces],
        compiler_params=params(),
        cost_estimate=cost(4 * n * toks * cols * width, n * toks * width * 4),
    )(own, *held_far, back)


def first_grads(groups, own, far, partial, partial_sib, turned, scales):
    toks, width = own.shape[1:]
    cols, both = partial.shape
    scale_keys, scale_back = scales
    pieces = [k for group in groups for k in group]
    n = len(pieces)
    held_far, part = parts_of(pieces, far)
    p = len(held_far)

    def body(own_ref, *refs):
        far_refs, (p_ref, q_ref, t_ref, k_ref), refs = refs[:p], refs[p : p + 4], refs[p + 4 :]
        for here, there in ((slice(0, toks), slice(toks, both)), (slice(toks, both), slice(0, toks))):
            value = (p_ref[:, here] + q_ref[:, there]) * scale_keys - t_ref[:, here]
            k_ref[:, here] = (value * scale_back).astype(bf16)
        for o_ref, group in zip(refs, groups):
            for slab, k in enumerate(group):
                value = jnp.dot(k_ref[:, :toks], own_ref[k], preferred_element_type=f32)
                block = far_refs[part[k]][k % PART]
                value += jnp.dot(k_ref[:, toks:], block, preferred_element_type=f32)
                o_ref[slab] = value.astype(bf16)

    return pl.pallas_call(
        body,
        in_specs=in_vmem(4 + p),
        out_specs=in_vmem(1 + len(groups)),
        out_shape=[jax.ShapeDtypeStruct((cols, both), bf16)]
        + [jax.ShapeDtypeStruct((len(group), cols, width), bf16) for group in groups],
        compiler_params=params(),
        cost_estimate=cost(4 * n * toks * cols * width, cols * toks * 28),
    )(own, *held_far, partial, partial_sib, turned)


def combine(rows, kind, *values):
    shape = values[0].shape[-2:]

    def body(*refs):
        def term(i, slab):
            ref = refs[i]
            return (ref[...] if len(ref.shape) == 2 else ref[slab]).astype(f32)

        for slab, terms in enumerate(rows):
            value = term(*terms[0])
            for extra in terms[1:]:
                value = value + term(*extra)
            refs[-1][slab] = value.astype(kind)

    return pl.pallas_call(
        body,
        in_specs=in_vmem(len(values)),
        out_specs=pl.BlockSpec(memory_space=VM),
        out_shape=jax.ShapeDtypeStruct((len(rows),) + shape, kind),
        compiler_params=params(),
        cost_estimate=cost(0, len(rows) * shape[0] * shape[1] * 8),
    )(*values)


def fragment_delta(fragment, outer, weight):
    rows, width = outer.shape
    cols = width // FRAGS

    def body(g_ref, o_ref, w_ref, d_ref):
        for q in range(FRAGS):
            at = slice(q * cols, (q + 1) * cols)

            @pl.when(g_ref[0] == q)
            def _():
                d_ref[...] = o_ref[:, at] - w_ref[:, at]

    return pl.pallas_call(
        body,
        in_specs=[SCALARS] + in_vmem(2),
        out_specs=pl.BlockSpec(memory_space=VM),
        out_shape=jax.ShapeDtypeStruct((rows, cols), f32),
        compiler_params=params(),
        cost_estimate=cost(0, rows * cols * 12),
    )(fragment, outer, weight)


def outer_step(fragment, summed, outer, moment, replicas):
    rows, width = outer.shape
    cols = width // FRAGS

    def body(g_ref, d_ref, o_ref, m_ref, oo_ref, mo_ref):
        mean = d_ref[...] / replicas
        for q in range(FRAGS):
            at = slice(q * cols, (q + 1) * cols)
            here = g_ref[0] == q
            old, mom = o_ref[:, at], m_ref[:, at]
            mom_new = 0.9 * mom + mean
            mo_ref[:, at] = jnp.where(here, mom_new, mom)
            oo_ref[:, at] = jnp.where(here, old - 0.7 * (mean + 0.9 * mom_new), old)

    return pl.pallas_call(
        body,
        in_specs=[SCALARS] + in_vmem(3),
        out_specs=in_vmem(2),
        out_shape=[jax.ShapeDtypeStruct((rows, width), f32)] * 2,
        compiler_params=params(),
        cost_estimate=cost(0, rows * width * 16),
    )(fragment, summed, outer, moment)


def inner_step(fragment, parts, weight, first, second, outer_out):
    rows, width = weight.shape
    cols = width // FRAGS

    def body(g_ref, p0, p1, p2, w_ref, f_ref, s_ref, o_ref, inner, fo_ref, so_ref):
        for q in range(FRAGS):
            at = slice(q * cols, (q + 1) * cols)
            turned = p0[0, at, :] + p1[0, at, :].astype(f32) + p2[1, at, :].astype(f32)
            grad = turned.T
            fn = 0.9 * f_ref[:, at] + 0.1 * grad
            sn = 0.95 * s_ref[:, at] + 0.05 * grad * grad
            update = fn / first_fix / (jnp.sqrt(sn / second_fix) + 1e-08)
            w = w_ref[:, at]
            stepped = w - 0.02 * (update + 0.1 * w)
            fo_ref[:, at] = fn
            so_ref[:, at] = sn
            inner[:, at] = jnp.where(g_ref[0] == q, 0.5 * stepped + 0.5 * o_ref[:, at], stepped)

    return pl.pallas_call(
        body,
        in_specs=[SCALARS] + in_vmem(7),
        out_specs=in_vmem(3),
        out_shape=[jax.ShapeDtypeStruct((rows, width), f32)] * 3,
        compiler_params=params(),
        cost_estimate=cost(0, rows * width * 38),
    )(fragment, *parts, weight, first, second, outer_out)


def shards(
    acts,
    doc_ids,
    target,
    inner_weight,
    adam_first,
    adam_second,
    outer_weight,
    outer_moment,
    fragment,
):
    tok_count = acts.shape[1]
    group_tokens = tok_count * lax.axis_size("fsdp")
    features = acts[0]
    weight = inner_weight[0]
    width = weight.shape[0]
    me = lax.axis_index("fsdp")
    c, z, x = me % 2, (me // 2) % NZ, me // (2 * NZ)

    def column_blocks(core):
        s = way(core)

        def at(dx, dz, other):
            half = 1 - core if other else core
            return ((x + dx) % NX * NZ + (z + dz) % NZ) * 2 + half

        order = [at(0, 0, 0), at(s, 0, 0), at(s, 0, 1), at(2, 0, 0)]
        order += [at(0, s, 0), at(0, s, 1), at(s, s, 0), at(s, s, 1), at(2, s, 0)]
        order += [at(s, -s, 0), at(s, -s, 1), at(2, -s, 0)]
        order += [at(0, 2, 0), at(s, 2, 0), at(s, 2, 1), at(2, 2, 0)]
        return jnp.stack(order).astype(jnp.int32)

    blocks, blocks_sib = column_blocks(c), column_blocks(1 - c)

    base = jnp.stack([me, me ^ 1]).astype(jnp.int32) * tok_count

    replicas = lax.axis_size("replica")
    summed = fragment_delta(fragment, outer_weight, weight)

    def swapped(value, step):
        return value + lax.ppermute(value, "replica", [(r, r ^ step) for r in range(replicas)])

    def pair(first, i, second, j):
        return combine([[(0, i)], [(1, j)]], bf16, first, second)

    def together(*values):
        return lax.optimization_barrier(values)

    a0 = turn_weight(weight, doc_ids, base)
    b0 = move(a0, SIBLING)
    S0 = pair(a0, 0, b0, 0)
    X0 = move(S0, FROM_X)
    Z1 = move(S0, FROM_Z)
    own, share = pick_columns(features, after(blocks, S0), blocks_sib, width)
    F0 = move(after(X0[0], own), FROM_X)
    X0, Z1, F0, own, summed, *share = together(X0, Z1, F0, own, summed, *share)

    C1 = move(Z1, SIBLING)
    X1 = move(Z1, FROM_X)
    a2 = move(Z1[0], FROM_Z)
    X2 = move(C1, FROM_X)
    far0 = move(after(share[0], C1), SIBLING)
    far1 = move(after(share[1], C1), SIBLING)
    b2 = move(after(a2, X1), SIBLING)
    X1, X2, a2, b2, far0, far1, *share = together(X1, X2, a2, b2, far0, far1, *share)

    F12 = move(pair(X1, 0, X2, 1), FROM_X)
    S3 = pair(a2, 0, b2, 0)
    X3 = move(S3, FROM_X)
    far2 = move(share[2], SIBLING)
    far3 = move(share[3], SIBLING)
    ids_sib = move(after(doc_ids, b2), SIBLING)
    target_sib = move(after(target[0], b2), SIBLING)
    far = (far0, far1, far2, far3)
    keys = add_keys([(0,), (1, 2), (3,)], own, far, (a0, X0, F0), None)
    keys = add_keys([(4, 5), (6, 7), (10, 9)], own, far, (Z1, X1, X2), keys)
    summed = swapped(after(summed, b2), 4)
    X3, F12, keys, ids_sib, target_sib, summed = together(
        X3, F12, keys, ids_sib, target_sib, summed
    )

    F2 = move(X3[0], FROM_X)
    keys = add_keys([(12,), (13, 14), (8, 11)], own, far, (a2, X3, F12), keys)
    F2, keys = together(F2, keys)
    notes = read_notes(a0, X0, F0, Z1, X1, X2, a2, X3, F12, F2)
    notes_sib = move(notes, SIBLING)
    partial = add_keys([(15,)], own, far, (after(F2, notes),), keys)
    partial_sib = move(after(partial, notes_sib), SIBLING)

    index = jnp.arange(HEAD // 2, dtype=f32)
    freqs = jnp.exp(index * f32(-2.0 * math.log(theta_base) / HEAD))[:, None]
    angles = token_angles(base, notes, notes_sib, doc_ids, ids_sib, freqs)
    turned = turn_target(target[0], target_sib, jnp.cos(angles), jnp.sin(angles))
    scales = (D ** (-0.5), group_tokens ** (-0.5))
    back, PF2 = first_grads(((15,),), own, far, partial, partial_sib, turned, scales)

    f2 = move(PF2, TO_X)
    PF1, P2 = grads([((8, 11), bf16), ((12, 13, 14), f32)], own, far, back)
    f1 = move(PF1, TO_X)
    summed = swapped(after(summed, back), 1)
    s2 = combine([[(0, 1), (1, 0)], [(0, 2)]], bf16, P2, f2)
    g2 = move(s2, TO_X)
    PM, PN = grads([((9, 10), f32), ((4, 5, 6, 7), f32)], own, far, after(back, s2))
    f1 = after(f1, PN, summed)
    s1 = combine([[(1, 3)], [(0, 0), (2, 1)], [(1, 2), (2, 0)], [(0, 1)]], bf16, PM, PN, f1)
    g1 = move(s1, TO_X)
    P0, PF0 = grads([((0, 1, 2), f32), ((3,), bf16)], own, far, after(back, s1))
    f0 = move(PF0, TO_X)
    g2, s1 = together(g2, s1)
    s3 = combine([[(0, 0), (1, 0), (2, 1)]], bf16, P2, g2, move(g2, SIBLING))
    u2 = move(s3, TO_Z)
    summed = swapped(after(summed, s3), 2)
    g1, u2, f0, summed = together(g1, u2, f0, summed)
    c1 = move(g1, SIBLING)
    s4 = combine(
        [[(0, 0), (1, 2), (2, 3), (3, 0)], [(0, 1), (1, 0), (2, 1)]], bf16, PN, g1, c1, u2
    )
    h = move(s4, TO_Z)
    s0 = combine([[(0, 1), (1, 0)], [(0, 2)]], bf16, P0, after(f0, s4))
    g0 = move(s0, TO_X)
    outer_out, moment_out = outer_step(
        fragment, after(summed, s0), outer_weight, outer_moment, replicas
    )
    g0, h = together(g0, h)
    mine = combine([[(0, 0), (1, 0), (2, 1)]], f32, P0, g0, move(g0, SIBLING))
    inner_out, first_out, second_out = inner_step(
        fragment, (mine, h, move(h, SIBLING)), weight, adam_first[0], adam_second[0], outer_out
    )
    return (inner_out[None], first_out[None], second_out[None], outer_out, moment_out)


def solution(mesh):
    in_specs = (
        P("replica", "fsdp", None),
        P("replica", "fsdp"),
        P("replica", "fsdp", None),
        P("replica", "fsdp", None),
        P("replica", "fsdp", None),
        P("replica", "fsdp", None),
        P("fsdp", None),
        P("fsdp", None),
        P(),
    )
    out_specs = (
        P("replica", "fsdp", None),
        P("replica", "fsdp", None),
        P("replica", "fsdp", None),
        P("fsdp", None),
        P("fsdp", None),
    )
    return jax.shard_map(shards, mesh=mesh, in_specs=in_specs, out_specs=out_specs, check_vma=False)
```

profile of v0, /device:TPU:1, one launch (start us, length us, event | category | flops | bytes accessed | tf_op | source)
XLA Modules:
  0.0 133.9 jit_solution(8852367469882838142)
XLA Ops:
  0.7 1.0 copy-done.1
  1.8 0.7 copy-done.9
  2.4 0.8 shard_map.128.refs_0_.refs_1_
  3.2 3.3 %collective-permute-start = (bf16[528,256]{1,0:T(8,128)(2,1)S(1)}, bf16[528,256]{1,0:T(8,128)(2,1)S(1)}, u32[]{:S(2)}, u32[]{:S(2)}) collective-permute-start(bf16[528,256]{1,0:T(8,128)(2,1)S(1)} %shard_map.128.refs_0_.refs_1_), channel_id=1, source_target_pairs={{0,1},{1,0},{2,3},{3,2},{4,5},{5,4},{6,7},{7,6},{8,9},{9,8},{10,11... | collective-permute-start | bytes 811016 | tf_op jit(solution)/shard_map/ppermute | solution.py:52
  6.6 1.2 collective-permute-done.refs_1_
  7.9 2.5 %collective-permute-start.2 = (bf16[2,528,256]{2,1,0:T(8,128)(2,1)S(1)}, bf16[2,528,256]{2,1,0:T(8,128)(2,1)S(1)}, u32[]{:S(2)}, u32[]{:S(2)}) collective-permute-start(bf16[2,528,256]{2,1,0:T(8,128)(2,1)S(1)} %shard_map.129), channel_id=1, source_target_pairs={{0,6},{1,3},{2,0},{3,5},{4,2},{5,7},{6,4},{7,1},{8,14},{9,11},{10,... | collective-permute-start | bytes 1622024 | tf_op jit(solution)/shard_map/ppermute | solution.py:52
  10.5 3.4 %copy-done = bf16[1,512,8192]{2,1,0:T(8,128)(2,1)S(1)} copy-done((bf16[1,512,8192]{2,1,0:T(8,128)(2,1)S(1)}, bf16[1,512,8192]{2,1,0:T(8,128)(2,1)}, u32[]{:S(2)}) %copy-start) | copy-done | bytes 8388632
  13.9 2.3 %shard_map.130 = (bf16[16,512,256]{2,1,0:T(8,128)(2,1)S(1)}, bf16[4,512,256]{2,1,0:T(8,128)(2,1)S(1)}, bf16[4,512,256]{2,1,0:T(8,128)(2,1)S(1)}, bf16[4,512,256]...) custom-call(s32[16]{0:T(128)S(1)} %stack.130.b_ref, s32[16]{0:T(128)S(1)} %stack.147.d_ref, bf16[512,8192]{1,0:T(8,128)(2,1)S(1)} %bitcast.48), custom_call_target="tpu_custom_call" | custom-call | bytes 16777216 | tf_op jit(solution)/shard_map/pallas_call | solution.py:194
  16.3 1.2 collective-permute-done.1.refs_2_.refs_1_
  18.3 3.8 %collective-permute-done.2.refs_2_.refs_3_ = bf16[2,528,256]{2,1,0:T(8,128)(2,1)S(1)} collective-permute-done((bf16[2,528,256]{2,1,0:T(8,128)(2,1)S(1)}, bf16[2,528,256]{2,1,0:T(8,128)(2,1)S(1)}, u32[]{:S(2)}, u32[]{:S(2)}) %collective-permute-start.2) | collective-permute-done | bytes 540704 | tf_op jit(solution)/shard_map/ppermute | solution.py:52
  22.1 2.1 %collective-permute-done.3.refs_3_.refs_2_ = bf16[528,256]{1,0:T(8,128)(2,1)S(1)} collective-permute-done((bf16[528,256]{1,0:T(8,128)(2,1)S(1)}, bf16[528,256]{1,0:T(8,128)(2,1)S(1)}, u32[]{:S(2)}, u32[]{:S(2)}) %collective-permute-start.3) | collective-permute-done | bytes 270368 | tf_op jit(solution)/shard_map/ppermute | solution.py:52
  24.2 4.1 %collective-permute-start.5 = (bf16[2,528,256]{2,1,0:T(8,128)(2,1)S(1)}, bf16[2,528,256]{2,1,0:T(8,128)(2,1)S(1)}, u32[]{:S(2)}, u32[]{:S(2)}) collective-permute-start(bf16[2,528,256]{2,1,0:T(8,128)(2,1)S(1)} %collective-permute-done.2.refs_2_.refs_3_), channel_id=1, source_target_pairs={{0,1},{1,0},{2,3},{3,2},{4,5},{5,4},{6,7},{7,6},{8,9},{9,8},{10,11... | collective-permute-start | bytes 1622024 | tf_op jit(solution)/shard_map/ppermute | solution.py:52
  28.3 1.6 %collective-permute-done.5 = bf16[2,528,256]{2,1,0:T(8,128)(2,1)S(1)} collective-permute-done((bf16[2,528,256]{2,1,0:T(8,128)(2,1)S(1)}, bf16[2,528,256]{2,1,0:T(8,128)(2,1)S(1)}, u32[]{:S(2)}, u32[]{:S(2)}) %collective-permute-start.5) | collective-permute-done | bytes 540704 | tf_op jit(solution)/shard_map/ppermute | solution.py:52
  29.8 0.4 collective-permute-start.10
  30.4 1.7 %collective-permute-start.7 = (bf16[528,256]{1,0:T(8,128)(2,1)S(1)}, bf16[528,256]{1,0:T(8,128)(2,1)S(1)}, u32[]{:S(2)}, u32[]{:S(2)}) collective-permute-start(bf16[528,256]{1,0:T(8,128)(2,1)S(1)} %slice_bitcast_fusion.2), channel_id=1, source_target_pairs={{0,6},{1,3},{2,0},{3,5},{4,2},{5,7},{6,4},{7,1},{8,14},{9,11},{10,... | collective-permute-start | bytes 811016 | tf_op jit(solution)/shard_map/ppermute | solution.py:52
  32.2 9.2 %collective-permute-done.7.refs_0_.refs_2_.refs_6_ = bf16[528,256]{1,0:T(8,128)(2,1)S(1)} collective-permute-done((bf16[528,256]{1,0:T(8,128)(2,1)S(1)}, bf16[528,256]{1,0:T(8,128)(2,1)S(1)}, u32[]{:S(2)}, u32[]{:S(2)}) %collective-permute-start.7) | collective-permute-done | bytes 270368 | tf_op jit(solution)/shard_map/ppermute | solution.py:52
  41.5 1.5 %collective-permute-start.8 = (bf16[528,256]{1,0:T(8,128)(2,1)S(1)}, bf16[528,256]{1,0:T(8,128)(2,1)S(1)}, u32[]{:S(2)}, u32[]{:S(2)}) collective-permute-start(bf16[528,256]{1,0:T(8,128)(2,1)S(1)} %collective-permute-done.7.refs_0_.refs_2_.refs_6_), channel_id=1, source_target_pairs={{0,1},{1,0},{2,3},{3,2},{4,5},{5,4},{6,7},{7,6},{8,9},{9,8},{10,11... | collective-permute-start | bytes 811016 | tf_op jit(solution)/shard_map/ppermute | solution.py:52
  42.9 1.2 collective-permute-done.8.refs_1_
  44.1 1.5 %collective-permute-done.6.refs_1_.refs_4_.refs_5_ = bf16[2,528,256]{2,1,0:T(8,128)(2,1)S(1)} collective-permute-done((bf16[2,528,256]{2,1,0:T(8,128)(2,1)S(1)}, bf16[2,528,256]{2,1,0:T(8,128)(2,1)S(1)}, u32[]{:S(2)}, u32[]{:S(2)}) %collective-permute-start.6) | collective-permute-done | bytes 540704 | tf_op jit(solution)/shard_map/ppermute | solution.py:52
  45.6 0.3 collective-permute-start.14
  46.1 0.6 collective-permute-start.17
  46.8 0.8 collective-permute-start.12
  47.6 3.3 %collective-permute-done.17 = f32[256,128]{1,0:T(8,128)S(1)} collective-permute-done((f32[256,128]{1,0:T(8,128)S(1)}, f32[256,128]{1,0:T(8,128)S(1)}, u32[]{:S(2)}, u32[]{:S(2)}) %collective-permute-start.17) | collective-permute-done | bytes 131104 | tf_op jit(solution)/shard_map/ppermute | solution.py:447
  50.9 1.1 collective-permute-start.16
  52.0 1.3 shard_map.134.refs_5_
  53.4 1.8 %shard_map.135.refs_5_ = f32[512,1024]{1,0:T(8,128)S(1)} custom-call(bf16[16,512,256]{2,1,0:T(8,128)(2,1)S(1)} %get-tuple-element.79.own_ref, bf16[4,512,256]{2,1,0:T(8,128)(2,1)S(1)} %collective-permute-done.10.refs_0_, bf16[4,512,256]{2,1,0:T(8,128)(2,1)S(1)} %collective-permute-done.14.refs_1_.refs_0_, ...), custom_call_target="tpu_custom_call" | custom-call | flops 1610612736 | bytes 2097152 | tf_op jit(solution)/shard_map/pallas_call | solution.py:240
  55.3 1.0 collective-permute-done.13.refs_4_.refs_8_
  56.3 5.8 %collective-permute-done.12.refs_3_.refs_7_ = bf16[2,528,256]{2,1,0:T(8,128)(2,1)S(1)} collective-permute-done((bf16[2,528,256]{2,1,0:T(8,128)(2,1)S(1)}, bf16[2,528,256]{2,1,0:T(8,128)(2,1)S(1)}, u32[]{:S(2)}, u32[]{:S(2)}) %collective-permute-start.12) | collective-permute-done | bytes 540704 | tf_op jit(solution)/shard_map/ppermute | solution.py:52
  62.2 1.6 %shard_map.136.refs_2_ = f32[512,1024]{1,0:T(8,128)S(1)} custom-call(bf16[16,512,256]{2,1,0:T(8,128)(2,1)S(1)} %get-tuple-element.79.own_ref, bf16[4,512,256]{2,1,0:T(8,128)(2,1)S(1)} %collective-permute-done.14.refs_1_.refs_0_, bf16[4,512,256]{2,1,0:T(8,128)(2,1)S(1)} %collective-permute-done.11.refs_1_.refs_0_, ...), custom_call_target="tpu_custom_call" | custom-call | flops 1342177280 | bytes 2097152 | tf_op jit(solution)/shard_map/pallas_call | solution.py:240
  63.8 4.9 %collective-permute-done.18.refs_9_.refs_1_ = bf16[528,256]{1,0:T(8,128)(2,1)S(1)} collective-permute-done((bf16[528,256]{1,0:T(8,128)(2,1)S(1)}, bf16[528,256]{1,0:T(8,128)(2,1)S(1)}, u32[]{:S(2)}, u32[]{:S(2)}) %collective-permute-start.18) | collective-permute-done | bytes 270368 | tf_op jit(solution)/shard_map/ppermute | solution.py:52
  68.8 2.3 %collective-permute-start.19 = (f32[8,256]{1,0:T(8,128)S(1)}, f32[8,256]{1,0:T(8,128)S(1)}, u32[]{:S(2)}, u32[]{:S(2)}) collective-permute-start(f32[8,256]{1,0:T(8,128)S(1)} %shard_map.137.n_ref), channel_id=1, source_target_pairs={{0,1},{1,0},{2,3},{3,2},{4,5},{5,4},{6,7},{7,6},{8,9},{9,8},{10,11... | collective-permute-start | bytes 24584 | tf_op jit(solution)/shard_map/ppermute | solution.py:52
  71.1 0.5 shard_map.138.refs_1_
  71.6 0.3 collective-permute-done.19.m_ref
  71.9 0.3 collective-permute-start.20
  72.3 0.6 shard_map.139
  72.9 1.0 fusion
  73.9 0.5 shard_map.140.refs_3_
  74.4 1.7 %collective-permute-done.20.refs_2_ = f32[512,1024]{1,0:T(8,128)S(1)} collective-permute-done((f32[512,1024]{1,0:T(8,128)S(1)}, f32[512,1024]{1,0:T(8,128)S(1)}, u32[]{:S(2)}, u32[]{:S(2)}) %collective-permute-start.20) | collective-permute-done | bytes 2097184 | tf_op jit(solution)/shard_map/ppermute | solution.py:52
  76.1 0.6 shard_map.141
  76.7 3.5 %collective-permute-start.21 = (bf16[1,512,256]{2,1,0:T(8,128)(2,1)S(1)}, bf16[1,512,256]{2,1,0:T(8,128)(2,1)S(1)}, u32[]{:S(2)}, u32[]{:S(2)}) collective-permute-start(bf16[1,512,256]{2,1,0:T(8,128)(2,1)S(1)} %get-tuple-element.113), channel_id=1, source_target_pairs={{0,8},{1,25},{2,10},{3,27},{4,12},{5,29},{6,14},{7,31},{8,16},{9,1... | collective-permute-start | bytes 786440 | tf_op jit(solution)/shard_map/ppermute | solution.py:52
  80.1 1.5 %shard_map.142 = (bf16[2,512,256]{2,1,0:T(8,128)(2,1)S(1)}, f32[3,512,256]{2,1,0:T(8,128)S(1)}) custom-call(bf16[16,512,256]{2,1,0:T(8,128)(2,1)S(1)} %get-tuple-element.79.own_ref, bf16[4,512,256]{2,1,0:T(8,128)(2,1)S(1)} %collective-permute-done.14.refs_1_.refs_0_, bf16[4,512,256]{2,1,0:T(8,128)(2,1)S(1)} %collective-permute-done.11.refs_1_.refs_0_, ...), custom_call_target="tpu_custom_call" | custom-call | flops 1342177280 | bytes 2621440 | tf_op jit(solution)/shard_map/pallas_call | solution.py:267
  81.8 1.4 %collective-permute-start.23 = (f32[256,128]{1,0:T(8,128)S(1)}, f32[256,128]{1,0:T(8,128)S(1)}, u32[]{:S(2)}, u32[]{:S(2)}) collective-permute-start(f32[256,128]{1,0:T(8,128)S(1)} %add.400), channel_id=1, source_target_pairs={{0,32},{32,0},{64,96},{96,64},{128,160},{160,128},{192,224},{224,1... | collective-permute-start | bytes 393224 | tf_op jit(solution)/shard_map/ppermute | solution.py:447
  83.5 3.4 %collective-permute-start.25 = (bf16[2,512,256]{2,1,0:T(8,128)(2,1)S(1)}, bf16[2,512,256]{2,1,0:T(8,128)(2,1)S(1)}, u32[]{:S(2)}, u32[]{:S(2)}) collective-permute-start(bf16[2,512,256]{2,1,0:T(8,128)(2,1)S(1)} %shard_map.143), channel_id=1, source_target_pairs={{0,8},{1,25},{2,10},{3,27},{4,12},{5,29},{6,14},{7,31},{8,16},{9,1... | collective-permute-start | bytes 1572872 | tf_op jit(solution)/shard_map/ppermute | solution.py:52
  87.0 1.8 %shard_map.144 = (f32[2,512,256]{2,1,0:T(8,128)S(1)}, f32[4,512,256]{2,1,0:T(8,128)S(1)}) custom-call(bf16[16,512,256]{2,1,0:T(8,128)(2,1)S(1)} %get-tuple-element.79.own_ref, bf16[4,512,256]{2,1,0:T(8,128)(2,1)S(1)} %collective-permute-done.10.refs_0_, bf16[4,512,256]{2,1,0:T(8,128)(2,1)S(1)} %collective-permute-done.14.refs_1_.refs_0_, ...), custom_call_target="tpu_custom_call" | custom-call | flops 1610612736 | bytes 3145728 | tf_op jit(solution)/shard_map/pallas_call | solution.py:267
  88.8 1.3 collective-permute-done.22.refs_2_
  90.2 2.2 %collective-permute-start.24 = (bf16[4,512,256]{2,1,0:T(8,128)(2,1)S(1)}, bf16[4,512,256]{2,1,0:T(8,128)(2,1)S(1)}, u32[]{:S(2)}, u32[]{:S(2)}) collective-permute-start(bf16[4,512,256]{2,1,0:T(8,128)(2,1)S(1)} %shard_map.145), channel_id=1, source_target_pairs={{0,8},{1,25},{2,10},{3,27},{4,12},{5,29},{6,14},{7,31},{8,16},{9,1... | collective-permute-start | bytes 3145736 | tf_op jit(solution)/shard_map/ppermute | solution.py:52
  92.4 3.3 %collective-permute-done.25.refs_1_ = bf16[2,512,256]{2,1,0:T(8,128)(2,1)S(1)} collective-permute-done((bf16[2,512,256]{2,1,0:T(8,128)(2,1)S(1)}, bf16[2,512,256]{2,1,0:T(8,128)(2,1)S(1)}, u32[]{:S(2)}, u32[]{:S(2)}) %collective-permute-start.25) | collective-permute-done | bytes 524320 | tf_op jit(solution)/shard_map/ppermute | solution.py:52
  95.7 0.7 collective-permute-start.26
  96.4 1.3 shard_map.146
  97.6 1.8 %collective-permute-start.28 = (bf16[1,512,256]{2,1,0:T(8,128)(2,1)S(1)}, bf16[1,512,256]{2,1,0:T(8,128)(2,1)S(1)}, u32[]{:S(2)}, u32[]{:S(2)}) collective-permute-start(bf16[1,512,256]{2,1,0:T(8,128)(2,1)S(1)} %get-tuple-element.124), channel_id=1, source_target_pairs={{0,8},{1,25},{2,10},{3,27},{4,12},{5,29},{6,14},{7,31},{8,16},{9,1... | collective-permute-start | bytes 786440 | tf_op jit(solution)/shard_map/ppermute | solution.py:52
  99.5 3.6 %collective-permute-start.27 = (bf16[1,512,256]{2,1,0:T(8,128)(2,1)S(1)}, bf16[1,512,256]{2,1,0:T(8,128)(2,1)S(1)}, u32[]{:S(2)}, u32[]{:S(2)}) collective-permute-start(bf16[1,512,256]{2,1,0:T(8,128)(2,1)S(1)} %shard_map.147), channel_id=1, source_target_pairs={{0,2},{1,7},{2,4},{3,1},{4,6},{5,3},{6,0},{7,5},{8,10},{9,15},{10,... | collective-permute-start | bytes 786440 | tf_op jit(solution)/shard_map/ppermute | solution.py:52
  103.2 2.9 %collective-permute-start.29 = (f32[256,128]{1,0:T(8,128)S(1)}, f32[256,128]{1,0:T(8,128)S(1)}, u32[]{:S(2)}, u32[]{:S(2)}) collective-permute-start(f32[256,128]{1,0:T(8,128)S(1)} %add.401), channel_id=1, source_target_pairs={{0,64},{32,96},{64,0},{96,32},{128,192},{160,224},{192,128},{224,1... | collective-permute-start | bytes 393224 | tf_op jit(solution)/shard_map/ppermute | solution.py:447
  106.1 2.4 %collective-permute-done.29 = f32[256,128]{1,0:T(8,128)S(1)} collective-permute-done((f32[256,128]{1,0:T(8,128)S(1)}, f32[256,128]{1,0:T(8,128)S(1)}, u32[]{:S(2)}, u32[]{:S(2)}) %collective-permute-start.29) | collective-permute-done | bytes 131104 | tf_op jit(solution)/shard_map/ppermute | solution.py:447
  108.5 1.2 collective-permute-done.28.refs_1_
  109.8 0.7 collective-permute-start.30
  110.4 2.3 %collective-permute-done.30.refs_2_ = bf16[4,512,256]{2,1,0:T(8,128)(2,1)S(1)} collective-permute-done((bf16[4,512,256]{2,1,0:T(8,128)(2,1)S(1)}, bf16[4,512,256]{2,1,0:T(8,128)(2,1)S(1)}, u32[]{:S(2)}, u32[]{:S(2)}) %collective-permute-start.30) | collective-permute-done | bytes 1048608 | tf_op jit(solution)/shard_map/ppermute | solution.py:52
  113.0 1.9 %collective-permute-start.31 = (bf16[2,512,256]{2,1,0:T(8,128)(2,1)S(1)}, bf16[2,512,256]{2,1,0:T(8,128)(2,1)S(1)}, u32[]{:S(2)}, u32[]{:S(2)}) collective-permute-start(bf16[2,512,256]{2,1,0:T(8,128)(2,1)S(1)} %shard_map.149), channel_id=1, source_target_pairs={{0,8},{1,25},{2,10},{3,27},{4,12},{5,29},{6,14},{7,31},{8,16},{9,1... | collective-permute-start | bytes 1572872 | tf_op jit(solution)/shard_map/ppermute | solution.py:52
  114.9 3.5 %collective-permute-start.32 = (bf16[2,512,256]{2,1,0:T(8,128)(2,1)S(1)}, bf16[2,512,256]{2,1,0:T(8,128)(2,1)S(1)}, u32[]{:S(2)}, u32[]{:S(2)}) collective-permute-start(bf16[2,512,256]{2,1,0:T(8,128)(2,1)S(1)} %shard_map.148), channel_id=1, source_target_pairs={{0,2},{1,7},{2,4},{3,1},{4,6},{5,3},{6,0},{7,5},{8,10},{9,15},{10,... | collective-permute-start | bytes 1572872 | tf_op jit(solution)/shard_map/ppermute | solution.py:52
  118.5 2.9 %collective-permute-done.31.refs_1_ = bf16[2,512,256]{2,1,0:T(8,128)(2,1)S(1)} collective-permute-done((bf16[2,512,256]{2,1,0:T(8,128)(2,1)S(1)}, bf16[2,512,256]{2,1,0:T(8,128)(2,1)S(1)}, u32[]{:S(2)}, u32[]{:S(2)}) %collective-permute-start.31) | collective-permute-done | bytes 524320 | tf_op jit(solution)/shard_map/ppermute | solution.py:52
  121.4 8.1 %collective-permute-done.32.p1 = bf16[2,512,256]{2,1,0:T(8,128)(2,1)S(1)} collective-permute-done((bf16[2,512,256]{2,1,0:T(8,128)(2,1)S(1)}, bf16[2,512,256]{2,1,0:T(8,128)(2,1)S(1)}, u32[]{:S(2)}, u32[]{:S(2)}) %collective-permute-start.32) | collective-permute-done | bytes 524320 | tf_op jit(solution)/shard_map/ppermute | solution.py:52
  129.5 0.5 collective-permute-start.34
  130.0 1.2 shard_map.151
  131.5 0.7 collective-permute-done.34.p2
  132.2 1.7 %shard_map.152 = (f32[256,512]{1,0:T(8,128)}, f32[256,512]{1,0:T(8,128)}, f32[256,512]{1,0:T(8,128)}) custom-call(s32[1]{0:T(128)S(6)} %copy.14.g_ref, f32[1,512,256]{2,1,0:T(8,128)S(1)} %shard_map.150.p0, bf16[2,512,256]{2,1,0:T(8,128)(2,1)S(1)} %collective-permute-done.32.p1, bf16[2,512,256]{2,1,0:T(8,128)(2,1)S(1)} %collective-permute-done.34.p2, ...), custom_call_target="tpu_custom_call" | custom-call | bytes 4980736 | tf_op jit(solution)/shard_map/pallas_call | solution.py:397
  (64 shorter events, 3.0 us)
Async XLA Ops:
  0.7 1.0 copy-start.1
  1.8 0.7 copy-start.9
  3.2 4.5 %collective-permute-start = (bf16[528,256]{1,0:T(8,128)(2,1)S(1)}, bf16[528,256]{1,0:T(8,128)(2,1)S(1)}, u32[]{:S(2)}, u32[]{:S(2)}) collective-permute-start(bf16[528,256]{1,0:T(8,128)(2,1)S(1)} %shard_map.128.refs_0_.refs_1_), channel_id=1, source_target_pairs={{0,1},{1,0},{2,3},{3,2},{4,5},{5,4},{6,7},{7,6},{8,9},{9,8},{10,11... | collective-permute-start | bytes 811016 | tf_op jit(solution)/shard_map/ppermute | solution.py:52
  7.8 9.6 %collective-permute-start.1 = (bf16[2,528,256]{2,1,0:T(8,128)(2,1)S(1)}, bf16[2,528,256]{2,1,0:T(8,128)(2,1)S(1)}, u32[]{:S(2)}, u32[]{:S(2)}) collective-permute-start(bf16[2,528,256]{2,1,0:T(8,128)(2,1)S(1)} %shard_map.129), channel_id=1, source_target_pairs={{0,24},{1,9},{2,26},{3,11},{4,28},{5,13},{6,30},{7,15},{8,0},{9,17... | collective-permute-start | bytes 1622024 | tf_op jit(solution)/shard_map/ppermute | solution.py:52
  7.9 14.2 %collective-permute-start.2 = (bf16[2,528,256]{2,1,0:T(8,128)(2,1)S(1)}, bf16[2,528,256]{2,1,0:T(8,128)(2,1)S(1)}, u32[]{:S(2)}, u32[]{:S(2)}) collective-permute-start(bf16[2,528,256]{2,1,0:T(8,128)(2,1)S(1)} %shard_map.129), channel_id=1, source_target_pairs={{0,6},{1,3},{2,0},{3,5},{4,2},{5,7},{6,4},{7,1},{8,14},{9,11},{10,... | collective-permute-start | bytes 1622024 | tf_op jit(solution)/shard_map/ppermute | solution.py:52
  10.5 3.4 %copy-start = (bf16[1,512,8192]{2,1,0:T(8,128)(2,1)S(1)}, bf16[1,512,8192]{2,1,0:T(8,128)(2,1)}, u32[]{:S(2)}) copy-start(bf16[1,512,8192]{2,1,0:T(8,128)(2,1)} %param.9) | copy-start | bytes 25165828
  13.9 4.3 %copy-start.2 = (f32[1,256,512]{2,1,0:T(8,128)S(1)}, f32[1,256,512]{2,1,0:T(8,128)}, u32[]{:S(2)}) copy-start(f32[1,256,512]{2,1,0:T(8,128)} %param.12) | copy-start | bytes 1572868
  13.9 4.3 %copy-start.3 = (f32[256,512]{1,0:T(8,128)S(1)}, f32[256,512]{1,0:T(8,128)}, u32[]{:S(2)}) copy-start(f32[256,512]{1,0:T(8,128)} %o_ref.3) | copy-start | bytes 1572868
  17.4 6.7 %collective-permute-start.3 = (bf16[528,256]{1,0:T(8,128)(2,1)S(1)}, bf16[528,256]{1,0:T(8,128)(2,1)S(1)}, u32[]{:S(2)}, u32[]{:S(2)}) collective-permute-start(bf16[528,256]{1,0:T(8,128)(2,1)S(1)} %slice_bitcast_fusion), channel_id=1, source_target_pairs={{0,24},{1,9},{2,26},{3,11},{4,28},{5,13},{6,30},{7,15},{8,0},{9,17... | collective-permute-start | bytes 811016 | tf_op jit(solution)/shard_map/ppermute | solution.py:52
  18.3 32.6 %copy-start.4 = (bf16[1,512,512]{2,1,0:T(8,128)(2,1)S(1)}, bf16[1,512,512]{2,1,0:T(8,128)(2,1)}, u32[]{:S(2)}) copy-start(bf16[1,512,512]{2,1,0:T(8,128)(2,1)} %param.11) | copy-start | bytes 1572868
  24.2 5.6 %collective-permute-start.5 = (bf16[2,528,256]{2,1,0:T(8,128)(2,1)S(1)}, bf16[2,528,256]{2,1,0:T(8,128)(2,1)S(1)}, u32[]{:S(2)}, u32[]{:S(2)}) collective-permute-start(bf16[2,528,256]{2,1,0:T(8,128)(2,1)S(1)} %collective-permute-done.2.refs_2_.refs_3_), channel_id=1, source_target_pairs={{0,1},{1,0},{2,3},{3,2},{4,5},{5,4},{6,7},{7,6},{8,9},{9,8},{10,11... | collective-permute-start | bytes 1622024 | tf_op jit(solution)/shard_map/ppermute | solution.py:52
  29.8 15.7 %collective-permute-start.10 = (bf16[4,512,256]{2,1,0:T(8,128)(2,1)S(1)}, bf16[4,512,256]{2,1,0:T(8,128)(2,1)S(1)}, u32[]{:S(2)}, u32[]{:S(2)}) collective-permute-start(bf16[4,512,256]{2,1,0:T(8,128)(2,1)S(1)} %get-tuple-element.85), channel_id=1, source_target_pairs={{0,1},{1,0},{2,3},{3,2},{4,5},{5,4},{6,7},{7,6},{8,9},{9,8},{10,11... | collective-permute-start | bytes 3145736 | tf_op jit(solution)/shard_map/ppermute | solution.py:52
  30.2 15.4 %collective-permute-start.9 = (bf16[4,512,256]{2,1,0:T(8,128)(2,1)S(1)}, bf16[4,512,256]{2,1,0:T(8,128)(2,1)S(1)}, u32[]{:S(2)}, u32[]{:S(2)}) collective-permute-start(bf16[4,512,256]{2,1,0:T(8,128)(2,1)S(1)} %get-tuple-element.83), channel_id=1, source_target_pairs={{0,1},{1,0},{2,3},{3,2},{4,5},{5,4},{6,7},{7,6},{8,9},{9,8},{10,11... | collective-permute-start | bytes 3145736 | tf_op jit(solution)/shard_map/ppermute | solution.py:52
  30.3 11.1 %collective-permute-start.4 = (bf16[2,528,256]{2,1,0:T(8,128)(2,1)S(1)}, bf16[2,528,256]{2,1,0:T(8,128)(2,1)S(1)}, u32[]{:S(2)}, u32[]{:S(2)}) collective-permute-start(bf16[2,528,256]{2,1,0:T(8,128)(2,1)S(1)} %collective-permute-done.2.refs_2_.refs_3_), channel_id=1, source_target_pairs={{0,24},{1,9},{2,26},{3,11},{4,28},{5,13},{6,30},{7,15},{8,0},{9,17... | collective-permute-start | bytes 1622024 | tf_op jit(solution)/shard_map/ppermute | solution.py:52
  30.4 11.1 %collective-permute-start.7 = (bf16[528,256]{1,0:T(8,128)(2,1)S(1)}, bf16[528,256]{1,0:T(8,128)(2,1)S(1)}, u32[]{:S(2)}, u32[]{:S(2)}) collective-permute-start(bf16[528,256]{1,0:T(8,128)(2,1)S(1)} %slice_bitcast_fusion.2), channel_id=1, source_target_pairs={{0,6},{1,3},{2,0},{3,5},{4,2},{5,7},{6,4},{7,1},{8,14},{9,11},{10,... | collective-permute-start | bytes 811016 | tf_op jit(solution)/shard_map/ppermute | solution.py:52
  32.0 13.5 %collective-permute-start.6 = (bf16[2,528,256]{2,1,0:T(8,128)(2,1)S(1)}, bf16[2,528,256]{2,1,0:T(8,128)(2,1)S(1)}, u32[]{:S(2)}, u32[]{:S(2)}) collective-permute-start(bf16[2,528,256]{2,1,0:T(8,128)(2,1)S(1)} %collective-permute-done.5), channel_id=1, source_target_pairs={{0,24},{1,9},{2,26},{3,11},{4,28},{5,13},{6,30},{7,15},{8,0},{9,17... | collective-permute-start | bytes 1622024 | tf_op jit(solution)/shard_map/ppermute | solution.py:52
  41.5 2.6 %collective-permute-start.8 = (bf16[528,256]{1,0:T(8,128)(2,1)S(1)}, bf16[528,256]{1,0:T(8,128)(2,1)S(1)}, u32[]{:S(2)}, u32[]{:S(2)}) collective-permute-start(bf16[528,256]{1,0:T(8,128)(2,1)S(1)} %collective-permute-done.7.refs_0_.refs_2_.refs_6_), channel_id=1, source_target_pairs={{0,1},{1,0},{2,3},{3,2},{4,5},{5,4},{6,7},{7,6},{8,9},{9,8},{10,11... | collective-permute-start | bytes 811016 | tf_op jit(solution)/shard_map/ppermute | solution.py:52
  45.6 7.7 %collective-permute-start.14 = (bf16[4,512,256]{2,1,0:T(8,128)(2,1)S(1)}, bf16[4,512,256]{2,1,0:T(8,128)(2,1)S(1)}, u32[]{:S(2)}, u32[]{:S(2)}) collective-permute-start(bf16[4,512,256]{2,1,0:T(8,128)(2,1)S(1)} %get-tuple-element.95), channel_id=1, source_target_pairs={{0,1},{1,0},{2,3},{3,2},{4,5},{5,4},{6,7},{7,6},{8,9},{9,8},{10,11... | collective-permute-start | bytes 3145736 | tf_op jit(solution)/shard_map/ppermute | solution.py:52
  45.9 16.3 %collective-permute-start.11 = (bf16[4,512,256]{2,1,0:T(8,128)(2,1)S(1)}, bf16[4,512,256]{2,1,0:T(8,128)(2,1)S(1)}, u32[]{:S(2)}, u32[]{:S(2)}) collective-permute-start(bf16[4,512,256]{2,1,0:T(8,128)(2,1)S(1)} %get-tuple-element.89), channel_id=1, source_target_pairs={{0,1},{1,0},{2,3},{3,2},{4,5},{5,4},{6,7},{7,6},{8,9},{9,8},{10,11... | collective-permute-start | bytes 3145736 | tf_op jit(solution)/shard_map/ppermute | solution.py:52
  46.1 4.8 %collective-permute-start.17 = (f32[256,128]{1,0:T(8,128)S(1)}, f32[256,128]{1,0:T(8,128)S(1)}, u32[]{:S(2)}, u32[]{:S(2)}) collective-permute-start(f32[256,128]{1,0:T(8,128)S(1)} %shard_map.131), channel_id=1, source_target_pairs={{0,128},{32,160},{64,192},{96,224},{128,0},{160,32},{192,64},{224,... | collective-permute-start | bytes 393224 | tf_op jit(solution)/shard_map/ppermute | solution.py:447
  46.7 9.6 %collective-permute-start.13 = (bf16[2,528,256]{2,1,0:T(8,128)(2,1)S(1)}, bf16[2,528,256]{2,1,0:T(8,128)(2,1)S(1)}, u32[]{:S(2)}, u32[]{:S(2)}) collective-permute-start(bf16[2,528,256]{2,1,0:T(8,128)(2,1)S(1)} %shard_map.133), channel_id=1, source_target_pairs={{0,24},{1,9},{2,26},{3,11},{4,28},{5,13},{6,30},{7,15},{8,0},{9,17... | collective-permute-start | bytes 1622024 | tf_op jit(solution)/shard_map/ppermute | solution.py:52
  46.8 15.3 %collective-permute-start.12 = (bf16[2,528,256]{2,1,0:T(8,128)(2,1)S(1)}, bf16[2,528,256]{2,1,0:T(8,128)(2,1)S(1)}, u32[]{:S(2)}, u32[]{:S(2)}) collective-permute-start(bf16[2,528,256]{2,1,0:T(8,128)(2,1)S(1)} %shard_map.132), channel_id=1, source_target_pairs={{0,24},{1,9},{2,26},{3,11},{4,28},{5,13},{6,30},{7,15},{8,0},{9,17... | collective-permute-start | bytes 1622024 | tf_op jit(solution)/shard_map/ppermute | solution.py:52
  47.6 5.7 %copy-start.10 = (s32[1,512]{1,0:T(1,128)S(1)}, s32[1,512]{1,0:T(1,128)}, u32[]{:S(2)}) copy-start(s32[1,512]{1,0:T(1,128)} %i_ref.3) | copy-start | bytes 6148
  50.9 4.4 %collective-permute-start.16 = (bf16[512,512]{1,0:T(8,128)(2,1)S(1)}, bf16[512,512]{1,0:T(8,128)(2,1)S(1)}, u32[]{:S(2)}, u32[]{:S(2)}) collective-permute-start(bf16[512,512]{1,0:T(8,128)(2,1)S(1)} %bitcast.52), channel_id=1, source_target_pairs={{0,1},{1,0},{2,3},{3,2},{4,5},{5,4},{6,7},{7,6},{8,9},{9,8},{10,11... | collective-permute-start | bytes 1572872 | tf_op jit(solution)/shard_map/ppermute | solution.py:52
  53.3 1.9 %collective-permute-start.15 = (s32[1,512]{1,0:T(1,128)S(1)}, s32[1,512]{1,0:T(1,128)S(1)}, u32[]{:S(2)}, u32[]{:S(2)}) collective-permute-start(s32[1,512]{1,0:T(1,128)S(1)} %copy-done.10), channel_id=1, source_target_pairs={{0,1},{1,0},{2,3},{3,2},{4,5},{5,4},{6,7},{7,6},{8,9},{9,8},{10,11... | collective-permute-start | bytes 6152 | tf_op jit(solution)/shard_map/ppermute | solution.py:52
  62.1 6.6 %collective-permute-start.18 = (bf16[528,256]{1,0:T(8,128)(2,1)S(1)}, bf16[528,256]{1,0:T(8,128)(2,1)S(1)}, u32[]{:S(2)}, u32[]{:S(2)}) collective-permute-start(bf16[528,256]{1,0:T(8,128)(2,1)S(1)} %slice_bitcast_fusion.1), channel_id=1, source_target_pairs={{0,24},{1,9},{2,26},{3,11},{4,28},{5,13},{6,30},{7,15},{8,0},{9,17... | collective-permute-start | bytes 811016 | tf_op jit(solution)/shard_map/ppermute | solution.py:52
  68.8 3.2 %collective-permute-start.19 = (f32[8,256]{1,0:T(8,128)S(1)}, f32[8,256]{1,0:T(8,128)S(1)}, u32[]{:S(2)}, u32[]{:S(2)}) collective-permute-start(f32[8,256]{1,0:T(8,128)S(1)} %shard_map.137.n_ref), channel_id=1, source_target_pairs={{0,1},{1,0},{2,3},{3,2},{4,5},{5,4},{6,7},{7,6},{8,9},{9,8},{10,11... | collective-permute-start | bytes 24584 | tf_op jit(solution)/shard_map/ppermute | solution.py:52
  71.9 4.2 %collective-permute-start.20 = (f32[512,1024]{1,0:T(8,128)S(1)}, f32[512,1024]{1,0:T(8,128)S(1)}, u32[]{:S(2)}, u32[]{:S(2)}) collective-permute-start(f32[512,1024]{1,0:T(8,128)S(1)} %shard_map.138.refs_1_), channel_id=1, source_target_pairs={{0,1},{1,0},{2,3},{3,2},{4,5},{5,4},{6,7},{7,6},{8,9},{9,8},{10,11... | collective-permute-start | bytes 6291464 | tf_op jit(solution)/shard_map/ppermute | solution.py:52
  76.7 6.8 %collective-permute-start.21 = (bf16[1,512,256]{2,1,0:T(8,128)(2,1)S(1)}, bf16[1,512,256]{2,1,0:T(8,128)(2,1)S(1)}, u32[]{:S(2)}, u32[]{:S(2)}) collective-permute-start(bf16[1,512,256]{2,1,0:T(8,128)(2,1)S(1)} %get-tuple-element.113), channel_id=1, source_target_pairs={{0,8},{1,25},{2,10},{3,27},{4,12},{5,29},{6,14},{7,31},{8,16},{9,1... | collective-permute-start | bytes 786440 | tf_op jit(solution)/shard_map/ppermute | solution.py:52
  81.7 8.4 %collective-permute-start.22 = (bf16[2,512,256]{2,1,0:T(8,128)(2,1)S(1)}, bf16[2,512,256]{2,1,0:T(8,128)(2,1)S(1)}, u32[]{:S(2)}, u32[]{:S(2)}) collective-permute-start(bf16[2,512,256]{2,1,0:T(8,128)(2,1)S(1)} %get-tuple-element.117), channel_id=1, source_target_pairs={{0,8},{1,25},{2,10},{3,27},{4,12},{5,29},{6,14},{7,31},{8,16},{9,1... | collective-permute-start | bytes 1572872 | tf_op jit(solution)/shard_map/ppermute | solution.py:52
  81.8 5.2 %collective-permute-start.23 = (f32[256,128]{1,0:T(8,128)S(1)}, f32[256,128]{1,0:T(8,128)S(1)}, u32[]{:S(2)}, u32[]{:S(2)}) collective-permute-start(f32[256,128]{1,0:T(8,128)S(1)} %add.400), channel_id=1, source_target_pairs={{0,32},{32,0},{64,96},{96,64},{128,160},{160,128},{192,224},{224,1... | collective-permute-start | bytes 393224 | tf_op jit(solution)/shard_map/ppermute | solution.py:447
  83.5 12.2 %collective-permute-start.25 = (bf16[2,512,256]{2,1,0:T(8,128)(2,1)S(1)}, bf16[2,512,256]{2,1,0:T(8,128)(2,1)S(1)}, u32[]{:S(2)}, u32[]{:S(2)}) collective-permute-start(bf16[2,512,256]{2,1,0:T(8,128)(2,1)S(1)} %shard_map.143), channel_id=1, source_target_pairs={{0,8},{1,25},{2,10},{3,27},{4,12},{5,29},{6,14},{7,31},{8,16},{9,1... | collective-permute-start | bytes 1572872 | tf_op jit(solution)/shard_map/ppermute | solution.py:52
  90.2 19.5 %collective-permute-start.24 = (bf16[4,512,256]{2,1,0:T(8,128)(2,1)S(1)}, bf16[4,512,256]{2,1,0:T(8,128)(2,1)S(1)}, u32[]{:S(2)}, u32[]{:S(2)}) collective-permute-start(bf16[4,512,256]{2,1,0:T(8,128)(2,1)S(1)} %shard_map.145), channel_id=1, source_target_pairs={{0,8},{1,25},{2,10},{3,27},{4,12},{5,29},{6,14},{7,31},{8,16},{9,1... | collective-permute-start | bytes 3145736 | tf_op jit(solution)/shard_map/ppermute | solution.py:52
  95.7 3.8 %collective-permute-start.26 = (bf16[2,512,256]{2,1,0:T(8,128)(2,1)S(1)}, bf16[2,512,256]{2,1,0:T(8,128)(2,1)S(1)}, u32[]{:S(2)}, u32[]{:S(2)}) collective-permute-start(bf16[2,512,256]{2,1,0:T(8,128)(2,1)S(1)} %collective-permute-done.25.refs_1_), channel_id=1, source_target_pairs={{0,1},{1,0},{2,3},{3,2},{4,5},{5,4},{6,7},{7,6},{8,9},{9,8},{10,11... | collective-permute-start | bytes 1572872 | tf_op jit(solution)/shard_map/ppermute | solution.py:52
  97.6 12.1 %collective-permute-start.28 = (bf16[1,512,256]{2,1,0:T(8,128)(2,1)S(1)}, bf16[1,512,256]{2,1,0:T(8,128)(2,1)S(1)}, u32[]{:S(2)}, u32[]{:S(2)}) collective-permute-start(bf16[1,512,256]{2,1,0:T(8,128)(2,1)S(1)} %get-tuple-element.124), channel_id=1, source_target_pairs={{0,8},{1,25},{2,10},{3,27},{4,12},{5,29},{6,14},{7,31},{8,16},{9,1... | collective-permute-start | bytes 786440 | tf_op jit(solution)/shard_map/ppermute | solution.py:52
  99.5 10.2 %collective-permute-start.27 = (bf16[1,512,256]{2,1,0:T(8,128)(2,1)S(1)}, bf16[1,512,256]{2,1,0:T(8,128)(2,1)S(1)}, u32[]{:S(2)}, u32[]{:S(2)}) collective-permute-start(bf16[1,512,256]{2,1,0:T(8,128)(2,1)S(1)} %shard_map.147), channel_id=1, source_target_pairs={{0,2},{1,7},{2,4},{3,1},{4,6},{5,3},{6,0},{7,5},{8,10},{9,15},{10,... | collective-permute-start | bytes 786440 | tf_op jit(solution)/shard_map/ppermute | solution.py:52
  103.2 5.3 %collective-permute-start.29 = (f32[256,128]{1,0:T(8,128)S(1)}, f32[256,128]{1,0:T(8,128)S(1)}, u32[]{:S(2)}, u32[]{:S(2)}) collective-permute-start(f32[256,128]{1,0:T(8,128)S(1)} %add.401), channel_id=1, source_target_pairs={{0,64},{32,96},{64,0},{96,32},{128,192},{160,224},{192,128},{224,1... | collective-permute-start | bytes 393224 | tf_op jit(solution)/shard_map/ppermute | solution.py:447
  109.8 2.9 %collective-permute-start.30 = (bf16[4,512,256]{2,1,0:T(8,128)(2,1)S(1)}, bf16[4,512,256]{2,1,0:T(8,128)(2,1)S(1)}, u32[]{:S(2)}, u32[]{:S(2)}) collective-permute-start(bf16[4,512,256]{2,1,0:T(8,128)(2,1)S(1)} %collective-permute-done.24.refs_1_), channel_id=1, source_target_pairs={{0,1},{1,0},{2,3},{3,2},{4,5},{5,4},{6,7},{7,6},{8,9},{9,8},{10,11... | collective-permute-start | bytes 3145736 | tf_op jit(solution)/shard_map/ppermute | solution.py:52
  112.9 17.1 %copy-start.5 = (f32[256,512]{1,0:T(8,128)S(1)}, f32[256,512]{1,0:T(8,128)}, u32[]{:S(2)}) copy-start(f32[256,512]{1,0:T(8,128)} %m_ref.1) | copy-start | bytes 1572868
  113.0 19.1 %copy-start.6 = (f32[1,256,512]{2,1,0:T(8,128)S(1)}, f32[1,256,512]{2,1,0:T(8,128)}, u32[]{:S(2)}) copy-start(f32[1,256,512]{2,1,0:T(8,128)} %param.13) | copy-start | bytes 1572868
  113.0 19.1 %copy-start.7 = (f32[1,256,512]{2,1,0:T(8,128)S(1)}, f32[1,256,512]{2,1,0:T(8,128)}, u32[]{:S(2)}) copy-start(f32[1,256,512]{2,1,0:T(8,128)} %param.14) | copy-start | bytes 1572868
  113.0 8.4 %collective-permute-start.31 = (bf16[2,512,256]{2,1,0:T(8,128)(2,1)S(1)}, bf16[2,512,256]{2,1,0:T(8,128)(2,1)S(1)}, u32[]{:S(2)}, u32[]{:S(2)}) collective-permute-start(bf16[2,512,256]{2,1,0:T(8,128)(2,1)S(1)} %shard_map.149), channel_id=1, source_target_pairs={{0,8},{1,25},{2,10},{3,27},{4,12},{5,29},{6,14},{7,31},{8,16},{9,1... | collective-permute-start | bytes 1572872 | tf_op jit(solution)/shard_map/ppermute | solution.py:52
  114.9 14.6 %collective-permute-start.32 = (bf16[2,512,256]{2,1,0:T(8,128)(2,1)S(1)}, bf16[2,512,256]{2,1,0:T(8,128)(2,1)S(1)}, u32[]{:S(2)}, u32[]{:S(2)}) collective-permute-start(bf16[2,512,256]{2,1,0:T(8,128)(2,1)S(1)} %shard_map.148), channel_id=1, source_target_pairs={{0,2},{1,7},{2,4},{3,1},{4,6},{5,3},{6,0},{7,5},{8,10},{9,15},{10,... | collective-permute-start | bytes 1572872 | tf_op jit(solution)/shard_map/ppermute | solution.py:52
  129.5 1.9 %collective-permute-start.33 = (bf16[2,512,256]{2,1,0:T(8,128)(2,1)S(1)}, bf16[2,512,256]{2,1,0:T(8,128)(2,1)S(1)}, u32[]{:S(2)}, u32[]{:S(2)}) collective-permute-start(bf16[2,512,256]{2,1,0:T(8,128)(2,1)S(1)} %collective-permute-done.31.refs_1_), channel_id=1, source_target_pairs={{0,1},{1,0},{2,3},{3,2},{4,5},{5,4},{6,7},{7,6},{8,9},{9,8},{10,11... | collective-permute-start | bytes 1572872 | tf_op jit(solution)/shard_map/ppermute | solution.py:52
  129.5 2.7 %collective-permute-start.34 = (bf16[2,512,256]{2,1,0:T(8,128)(2,1)S(1)}, bf16[2,512,256]{2,1,0:T(8,128)(2,1)S(1)}, u32[]{:S(2)}, u32[]{:S(2)}) collective-permute-start(bf16[2,512,256]{2,1,0:T(8,128)(2,1)S(1)} %collective-permute-done.32.p1), channel_id=1, source_target_pairs={{0,1},{1,0},{2,3},{3,2},{4,5},{5,4},{6,7},{7,6},{8,9},{9,8},{10,11... | collective-permute-start | bytes 1572872 | tf_op jit(solution)/shard_map/ppermute | solution.py:52
  131.1 1.0 copy-start.8
where the time goes:
time: 134 us
  waiting for transfers between devices  61.4 us (46%)
  starting transfers between devices  46 us (34%)
  Pallas kernels  18.3 us (14%)
  local copies, waits for them, and re-layouts  6.39 us (5%)
  between operations  1.62 us (1%)
    ppermute x32, waiting for transfers between devices, move(): return lax.ppermute(value, 'fsdp', table)  55.7 us
    ppermute x32, starting transfers between devices, move(): return lax.ppermute(value, 'fsdp', table)  41.2 us
    ppermute x3, waiting for transfers between devices, swapped(): lax.ppermute(value, 'replica', [(r, r ^ step) for r in range(replicas)])  5.67 us
    unnamed x22, local copies, waits for them, and re-layouts  5.18 us
    pallas_call x4, Pallas kernels, add_keys(): pl.pallas_call(body, in_specs=in_vmem(1 + p + m + len(extra)), out_specs=...  5.17 us
    ppermute x3, starting transfers between devices, swapped(): lax.ppermute(value, 'replica', [(r, r ^ step) for r in range(replicas)])  4.86 us
    pallas_call x3, Pallas kernels, grads(): pl.pallas_call(body, in_specs=in_vmem(2 + p), out_specs=in_vmem(len(piece...  4.62 us
  transfers between devices with their start and end apart: 35, of which 24 were waited for; matrix products, arithmetic and copies ran while one was open for 1% of the time, Pallas kernels for 11%

commit v1 on v0

--- a/solution.py
+++ b/solution.py
@@ -211,7 +211,7 @@
     return [far[p] for p in used], {k: used.index(k // PART) for k in pieces}
 
 
-def add_keys(pieces, own, far, weights, total):
+def add_keys(pieces, own, far, weights, total, send=False):
     toks = own.shape[1]
     rows, width = weights[0].shape[-2:]
     cols = rows - NOTE
@@ -220,10 +220,11 @@
     n = len(names)
     held_far, part = parts_of(names, far)
     p = len(held_far)
+    extra = [] if total is None else [total]
 
     def body(own_ref, *refs):
         far_refs, refs = refs[:p], refs[p:]
-        o_ref = refs[-1]
+        o_ref = refs[m + len(extra)]
         values = [None, None]
         if total is not None:
             values = [refs[m][:, :toks], refs[m][:, toks:]]
@@ -235,16 +236,20 @@
                     values[j] = term if values[j] is None else values[j] + term
         o_ref[:, :toks] = values[0]
         o_ref[:, toks:] = values[1]
-
-    extra = [] if total is None else [total]
-    return pl.pallas_call(
+        if send:
+            refs[-1][:, :toks] = values[0].astype(bf16)
+            refs[-1][:, toks:] = values[1].astype(bf16)
+
+    kinds = [f32, bf16] if send else [f32]
+    out = pl.pallas_call(
         body,
         in_specs=in_vmem(1 + p + m + len(extra)),
-        out_specs=pl.BlockSpec(memory_space=VM),
-        out_shape=jax.ShapeDtypeStruct((cols, 2 * toks), f32),
+        out_specs=in_vmem(len(kinds)),
+        out_shape=[jax.ShapeDtypeStruct((cols, 2 * toks), kind) for kind in kinds],
         compiler_params=params(),
         cost_estimate=cost(4 * n * toks * cols * width, cols * toks * 8),
     )(own, *held_far, *weights, *extra)
+    return out if send else out[0]
 
 
 def grads(pieces, own, far, back):
@@ -286,7 +291,7 @@
     def body(own_ref, *refs):
         far_refs, (p_ref, q_ref, t_ref, k_ref), refs = refs[:p], refs[p : p + 4], refs[p + 4 :]
         for here, there in ((slice(0, toks), slice(toks, both)), (slice(toks, both), slice(0, toks))):
-            value = (p_ref[:, here] + q_ref[:, there]) * scale_keys - t_ref[:, here]
+            value = (p_ref[:, here] + q_ref[:, there].astype(f32)) * scale_keys - t_ref[:, here]
             k_ref[:, here] = (value * scale_back).astype(bf16)
         for o_ref, group in zip(refs, groups):
             for slab, k in enumerate(group):
@@ -490,8 +495,8 @@
     F2, keys = together(F2, keys)
     notes = read_notes(a0, X0, F0, Z1, X1, X2, a2, X3, F12, F2)
     notes_sib = move(notes, SIBLING)
-    partial = add_keys([(15,)], own, far, (after(F2, notes),), keys)
-    partial_sib = move(after(partial, notes_sib), SIBLING)
+    partial, rounded = add_keys([(15,)], own, far, (after(F2, notes),), keys, send=True)
+    partial_sib = move(after(rounded, notes_sib), SIBLING)
 
     index = jnp.arange(HEAD // 2, dtype=f32)
     freqs = jnp.exp(index * f32(-2.0 * math.log(theta_base) / HEAD))[:, None]

time: 134 us -> 133 us (level)
  waiting for transfers between devices: 61.4 us -> 59.9 us
    ppermute x32, waiting for transfers between devices: 55.7 us -> 54.2 us  [move(): return lax.ppermute(value, 'fsdp', table)]
where the time goes in v1:
time: 133 us; the launch traced here: 132 us
  waiting for transfers between devices  59.9 us (45%)
  starting transfers between devices  46 us (35%)
  Pallas kernels  18.3 us (14%)
  local copies, waits for them, and re-layouts  6.39 us (5%)
  between operations  1.62 us (1%)
    ppermute x32, waiting for transfers between devices, move(): return lax.ppermute(value, 'fsdp', table)  54.2 us
    ppermute x32, starting transfers between devices, move(): return lax.ppermute(value, 'fsdp', table)  41.2 us
    ppermute x3, waiting for transfers between devices, swapped(): lax.ppermute(value, 'replica', [(r, r ^ step) for r in range(replicas)])  5.67 us
    unnamed x22, local copies, waits for them, and re-layouts  5.18 us
    pallas_call x4, Pallas kernels, add_keys(): pl.pallas_call(body, in_specs=in_vmem(1 + p + m + len(extra)), out_specs=...  5.18 us
    ppermute x3, starting transfers between devices, swapped(): lax.ppermute(value, 'replica', [(r, r ^ step) for r in range(replicas)])  4.86 us
    pallas_call x3, Pallas kernels, grads(): pl.pallas_call(body, in_specs=in_vmem(2 + p), out_specs=in_vmem(len(piece...  4.62 us
  transfers between devices with their start and end apart: 35, of which 24 were waited for; matrix products, arithmetic and copies ran while one was open for 1% of the time, Pallas kernels for 11%

profile of v1, /device:TPU:1, one launch (start us, length us, event | category | flops | bytes accessed | tf_op | source)
XLA Modules:
  0.0 132.4 jit_solution(11943836179429736342)
XLA Ops:
  0.7 1.0 copy-done.1
  1.8 0.7 copy-done.9
  2.4 0.8 shard_map.128.refs_0_.refs_1_
  3.2 3.3 %collective-permute-start = (bf16[528,256]{1,0:T(8,128)(2,1)S(1)}, bf16[528,256]{1,0:T(8,128)(2,1)S(1)}, u32[]{:S(2)}, u32[]{:S(2)}) collective-permute-start(bf16[528,256]{1,0:T(8,128)(2,1)S(1)} %shard_map.128.refs_0_.refs_1_), channel_id=1, source_target_pairs={{0,1},{1,0},{2,3},{3,2},{4,5},{5,4},{6,7},{7,6},{8,9},{9,8},{10,11... | collective-permute-start | bytes 811016 | tf_op jit(solution)/shard_map/ppermute | solution.py:52
  6.6 1.2 collective-permute-done.refs_1_
  7.9 2.5 %collective-permute-start.2 = (bf16[2,528,256]{2,1,0:T(8,128)(2,1)S(1)}, bf16[2,528,256]{2,1,0:T(8,128)(2,1)S(1)}, u32[]{:S(2)}, u32[]{:S(2)}) collective-permute-start(bf16[2,528,256]{2,1,0:T(8,128)(2,1)S(1)} %shard_map.129), channel_id=1, source_target_pairs={{0,6},{1,3},{2,0},{3,5},{4,2},{5,7},{6,4},{7,1},{8,14},{9,11},{10,... | collective-permute-start | bytes 1622024 | tf_op jit(solution)/shard_map/ppermute | solution.py:52
  10.5 3.4 %copy-done = bf16[1,512,8192]{2,1,0:T(8,128)(2,1)S(1)} copy-done((bf16[1,512,8192]{2,1,0:T(8,128)(2,1)S(1)}, bf16[1,512,8192]{2,1,0:T(8,128)(2,1)}, u32[]{:S(2)}) %copy-start) | copy-done | bytes 8388632
  13.9 2.3 %shard_map.130 = (bf16[16,512,256]{2,1,0:T(8,128)(2,1)S(1)}, bf16[4,512,256]{2,1,0:T(8,128)(2,1)S(1)}, bf16[4,512,256]{2,1,0:T(8,128)(2,1)S(1)}, bf16[4,512,256]...) custom-call(s32[16]{0:T(128)S(1)} %stack.130.b_ref, s32[16]{0:T(128)S(1)} %stack.147.d_ref, bf16[512,8192]{1,0:T(8,128)(2,1)S(1)} %bitcast.48), custom_call_target="tpu_custom_call" | custom-call | bytes 16777216 | tf_op jit(solution)/shard_map/pallas_call | solution.py:194
  16.3 1.2 collective-permute-done.1.refs_2_.refs_1_
  18.3 3.8 %collective-permute-done.2.refs_2_.refs_3_ = bf16[2,528,256]{2,1,0:T(8,128)(2,1)S(1)} collective-permute-done((bf16[2,528,256]{2,1,0:T(8,128)(2,1)S(1)}, bf16[2,528,256]{2,1,0:T(8,128)(2,1)S(1)}, u32[]{:S(2)}, u32[]{:S(2)}) %collective-permute-start.2) | collective-permute-done | bytes 540704 | tf_op jit(solution)/shard_map/ppermute | solution.py:52
  22.1 2.1 %collective-permute-done.3.refs_3_.refs_2_ = bf16[528,256]{1,0:T(8,128)(2,1)S(1)} collective-permute-done((bf16[528,256]{1,0:T(8,128)(2,1)S(1)}, bf16[528,256]{1,0:T(8,128)(2,1)S(1)}, u32[]{:S(2)}, u32[]{:S(2)}) %collective-permute-start.3) | collective-permute-done | bytes 270368 | tf_op jit(solution)/shard_map/ppermute | solution.py:52
  24.2 4.1 %collective-permute-start.5 = (bf16[2,528,256]{2,1,0:T(8,128)(2,1)S(1)}, bf16[2,528,256]{2,1,0:T(8,128)(2,1)S(1)}, u32[]{:S(2)}, u32[]{:S(2)}) collective-permute-start(bf16[2,528,256]{2,1,0:T(8,128)(2,1)S(1)} %collective-permute-done.2.refs_2_.refs_3_), channel_id=1, source_target_pairs={{0,1},{1,0},{2,3},{3,2},{4,5},{5,4},{6,7},{7,6},{8,9},{9,8},{10,11... | collective-permute-start | bytes 1622024 | tf_op jit(solution)/shard_map/ppermute | solution.py:52
  28.3 1.6 %collective-permute-done.5 = bf16[2,528,256]{2,1,0:T(8,128)(2,1)S(1)} collective-permute-done((bf16[2,528,256]{2,1,0:T(8,128)(2,1)S(1)}, bf16[2,528,256]{2,1,0:T(8,128)(2,1)S(1)}, u32[]{:S(2)}, u32[]{:S(2)}) %collective-permute-start.5) | collective-permute-done | bytes 540704 | tf_op jit(solution)/shard_map/ppermute | solution.py:52
  29.8 0.4 collective-permute-start.10
  30.4 1.7 %collective-permute-start.7 = (bf16[528,256]{1,0:T(8,128)(2,1)S(1)}, bf16[528,256]{1,0:T(8,128)(2,1)S(1)}, u32[]{:S(2)}, u32[]{:S(2)}) collective-permute-start(bf16[528,256]{1,0:T(8,128)(2,1)S(1)} %slice_bitcast_fusion.2), channel_id=1, source_target_pairs={{0,6},{1,3},{2,0},{3,5},{4,2},{5,7},{6,4},{7,1},{8,14},{9,11},{10,... | collective-permute-start | bytes 811016 | tf_op jit(solution)/shard_map/ppermute | solution.py:52
  32.2 9.2 %collective-permute-done.7.refs_0_.refs_2_.refs_6_ = bf16[528,256]{1,0:T(8,128)(2,1)S(1)} collective-permute-done((bf16[528,256]{1,0:T(8,128)(2,1)S(1)}, bf16[528,256]{1,0:T(8,128)(2,1)S(1)}, u32[]{:S(2)}, u32[]{:S(2)}) %collective-permute-start.7) | collective-permute-done | bytes 270368 | tf_op jit(solution)/shard_map/ppermute | solution.py:52
  41.5 1.5 %collective-permute-start.8 = (bf16[528,256]{1,0:T(8,128)(2,1)S(1)}, bf16[528,256]{1,0:T(8,128)(2,1)S(1)}, u32[]{:S(2)}, u32[]{:S(2)}) collective-permute-start(bf16[528,256]{1,0:T(8,128)(2,1)S(1)} %collective-permute-done.7.refs_0_.refs_2_.refs_6_), channel_id=1, source_target_pairs={{0,1},{1,0},{2,3},{3,2},{4,5},{5,4},{6,7},{7,6},{8,9},{9,8},{10,11... | collective-permute-start | bytes 811016 | tf_op jit(solution)/shard_map/ppermute | solution.py:52
  42.9 1.2 collective-permute-done.8.refs_1_
  44.1 1.5 %collective-permute-done.6.refs_1_.refs_4_.refs_5_ = bf16[2,528,256]{2,1,0:T(8,128)(2,1)S(1)} collective-permute-done((bf16[2,528,256]{2,1,0:T(8,128)(2,1)S(1)}, bf16[2,528,256]{2,1,0:T(8,128)(2,1)S(1)}, u32[]{:S(2)}, u32[]{:S(2)}) %collective-permute-start.6) | collective-permute-done | bytes 540704 | tf_op jit(solution)/shard_map/ppermute | solution.py:52
  45.6 0.3 collective-permute-start.14
  46.1 0.6 collective-permute-start.17
  46.8 0.8 collective-permute-start.12
  47.6 3.3 %collective-permute-done.17 = f32[256,128]{1,0:T(8,128)S(1)} collective-permute-done((f32[256,128]{1,0:T(8,128)S(1)}, f32[256,128]{1,0:T(8,128)S(1)}, u32[]{:S(2)}, u32[]{:S(2)}) %collective-permute-start.17) | collective-permute-done | bytes 131104 | tf_op jit(solution)/shard_map/ppermute | solution.py:452
  50.9 1.1 collective-permute-start.16
  52.0 1.3 shard_map.134.refs_5_
  53.4 1.8 %shard_map.135.refs_5_ = f32[512,1024]{1,0:T(8,128)S(1)} custom-call(bf16[16,512,256]{2,1,0:T(8,128)(2,1)S(1)} %get-tuple-element.81.own_ref, bf16[4,512,256]{2,1,0:T(8,128)(2,1)S(1)} %collective-permute-done.10.refs_0_, bf16[4,512,256]{2,1,0:T(8,128)(2,1)S(1)} %collective-permute-done.14.refs_1_.refs_0_, ...), custom_call_target="tpu_custom_call" | custom-call | flops 1610612736 | bytes 2097152 | tf_op jit(solution)/shard_map/pallas_call | solution.py:244
  55.3 1.0 collective-permute-done.13.refs_4_.refs_8_
  56.3 5.8 %collective-permute-done.12.refs_3_.refs_7_ = bf16[2,528,256]{2,1,0:T(8,128)(2,1)S(1)} collective-permute-done((bf16[2,528,256]{2,1,0:T(8,128)(2,1)S(1)}, bf16[2,528,256]{2,1,0:T(8,128)(2,1)S(1)}, u32[]{:S(2)}, u32[]{:S(2)}) %collective-permute-start.12) | collective-permute-done | bytes 540704 | tf_op jit(solution)/shard_map/ppermute | solution.py:52
  62.2 1.6 %shard_map.136.refs_2_ = f32[512,1024]{1,0:T(8,128)S(1)} custom-call(bf16[16,512,256]{2,1,0:T(8,128)(2,1)S(1)} %get-tuple-element.81.own_ref, bf16[4,512,256]{2,1,0:T(8,128)(2,1)S(1)} %collective-permute-done.14.refs_1_.refs_0_, bf16[4,512,256]{2,1,0:T(8,128)(2,1)S(1)} %collective-permute-done.11.refs_1_.refs_0_, ...), custom_call_target="tpu_custom_call" | custom-call | flops 1342177280 | bytes 2097152 | tf_op jit(solution)/shard_map/pallas_call | solution.py:244
  63.8 4.9 %collective-permute-done.18.refs_9_.refs_1_ = bf16[528,256]{1,0:T(8,128)(2,1)S(1)} collective-permute-done((bf16[528,256]{1,0:T(8,128)(2,1)S(1)}, bf16[528,256]{1,0:T(8,128)(2,1)S(1)}, u32[]{:S(2)}, u32[]{:S(2)}) %collective-permute-start.18) | collective-permute-done | bytes 270368 | tf_op jit(solution)/shard_map/ppermute | solution.py:52
  68.8 2.3 %collective-permute-start.19 = (f32[8,256]{1,0:T(8,128)S(1)}, f32[8,256]{1,0:T(8,128)S(1)}, u32[]{:S(2)}, u32[]{:S(2)}) collective-permute-start(f32[8,256]{1,0:T(8,128)S(1)} %shard_map.137.n_ref), channel_id=1, source_target_pairs={{0,1},{1,0},{2,3},{3,2},{4,5},{5,4},{6,7},{7,6},{8,9},{9,8},{10,11... | collective-permute-start | bytes 24584 | tf_op jit(solution)/shard_map/ppermute | solution.py:52
  71.1 0.5 shard_map.138
  71.6 0.4 collective-permute-done.19.m_ref
  71.9 0.3 collective-permute-start.20
  72.3 0.6 shard_map.139
  72.9 1.0 fusion
  73.9 0.5 shard_map.140.refs_3_
  74.6 0.6 shard_map.141
  75.2 3.5 %collective-permute-start.21 = (bf16[1,512,256]{2,1,0:T(8,128)(2,1)S(1)}, bf16[1,512,256]{2,1,0:T(8,128)(2,1)S(1)}, u32[]{:S(2)}, u32[]{:S(2)}) collective-permute-start(bf16[1,512,256]{2,1,0:T(8,128)(2,1)S(1)} %get-tuple-element.117), channel_id=1, source_target_pairs={{0,8},{1,25},{2,10},{3,27},{4,12},{5,29},{6,14},{7,31},{8,16},{9,1... | collective-permute-start | bytes 786440 | tf_op jit(solution)/shard_map/ppermute | solution.py:52
  78.6 1.5 %shard_map.142 = (bf16[2,512,256]{2,1,0:T(8,128)(2,1)S(1)}, f32[3,512,256]{2,1,0:T(8,128)S(1)}) custom-call(bf16[16,512,256]{2,1,0:T(8,128)(2,1)S(1)} %get-tuple-element.81.own_ref, bf16[4,512,256]{2,1,0:T(8,128)(2,1)S(1)} %collective-permute-done.14.refs_1_.refs_0_, bf16[4,512,256]{2,1,0:T(8,128)(2,1)S(1)} %collective-permute-done.11.refs_1_.refs_0_, ...), custom_call_target="tpu_custom_call" | custom-call | flops 1342177280 | bytes 2621440 | tf_op jit(solution)/shard_map/pallas_call | solution.py:272
  80.3 1.4 %collective-permute-start.23 = (f32[256,128]{1,0:T(8,128)S(1)}, f32[256,128]{1,0:T(8,128)S(1)}, u32[]{:S(2)}, u32[]{:S(2)}) collective-permute-start(f32[256,128]{1,0:T(8,128)S(1)} %add.400), channel_id=1, source_target_pairs={{0,32},{32,0},{64,96},{96,64},{128,160},{160,128},{192,224},{224,1... | collective-permute-start | bytes 393224 | tf_op jit(solution)/shard_map/ppermute | solution.py:452
  81.7 0.3 collective-permute-done.21.refs_1_
  82.0 3.4 %collective-permute-start.25 = (bf16[2,512,256]{2,1,0:T(8,128)(2,1)S(1)}, bf16[2,512,256]{2,1,0:T(8,128)(2,1)S(1)}, u32[]{:S(2)}, u32[]{:S(2)}) collective-permute-start(bf16[2,512,256]{2,1,0:T(8,128)(2,1)S(1)} %shard_map.143), channel_id=1, source_target_pairs={{0,8},{1,25},{2,10},{3,27},{4,12},{5,29},{6,14},{7,31},{8,16},{9,1... | collective-permute-start | bytes 1572872 | tf_op jit(solution)/shard_map/ppermute | solution.py:52
  85.5 1.8 %shard_map.144 = (f32[2,512,256]{2,1,0:T(8,128)S(1)}, f32[4,512,256]{2,1,0:T(8,128)S(1)}) custom-call(bf16[16,512,256]{2,1,0:T(8,128)(2,1)S(1)} %get-tuple-element.81.own_ref, bf16[4,512,256]{2,1,0:T(8,128)(2,1)S(1)} %collective-permute-done.10.refs_0_, bf16[4,512,256]{2,1,0:T(8,128)(2,1)S(1)} %collective-permute-done.14.refs_1_.refs_0_, ...), custom_call_target="tpu_custom_call" | custom-call | flops 1610612736 | bytes 3145728 | tf_op jit(solution)/shard_map/pallas_call | solution.py:272
  87.3 1.3 collective-permute-done.22.refs_2_
  88.8 2.2 %collective-permute-start.24 = (bf16[4,512,256]{2,1,0:T(8,128)(2,1)S(1)}, bf16[4,512,256]{2,1,0:T(8,128)(2,1)S(1)}, u32[]{:S(2)}, u32[]{:S(2)}) collective-permute-start(bf16[4,512,256]{2,1,0:T(8,128)(2,1)S(1)} %shard_map.145), channel_id=1, source_target_pairs={{0,8},{1,25},{2,10},{3,27},{4,12},{5,29},{6,14},{7,31},{8,16},{9,1... | collective-permute-start | bytes 3145736 | tf_op jit(solution)/shard_map/ppermute | solution.py:52
  90.9 3.3 %collective-permute-done.25.refs_1_ = bf16[2,512,256]{2,1,0:T(8,128)(2,1)S(1)} collective-permute-done((bf16[2,512,256]{2,1,0:T(8,128)(2,1)S(1)}, bf16[2,512,256]{2,1,0:T(8,128)(2,1)S(1)}, u32[]{:S(2)}, u32[]{:S(2)}) %collective-permute-start.25) | collective-permute-done | bytes 524320 | tf_op jit(solution)/shard_map/ppermute | solution.py:52
  94.2 0.7 collective-permute-start.26
  94.9 1.3 shard_map.146
  96.1 1.8 %collective-permute-start.28 = (bf16[1,512,256]{2,1,0:T(8,128)(2,1)S(1)}, bf16[1,512,256]{2,1,0:T(8,128)(2,1)S(1)}, u32[]{:S(2)}, u32[]{:S(2)}) collective-permute-start(bf16[1,512,256]{2,1,0:T(8,128)(2,1)S(1)} %get-tuple-element.128), channel_id=1, source_target_pairs={{0,8},{1,25},{2,10},{3,27},{4,12},{5,29},{6,14},{7,31},{8,16},{9,1... | collective-permute-start | bytes 786440 | tf_op jit(solution)/shard_map/ppermute | solution.py:52
  98.1 3.6 %collective-permute-start.27 = (bf16[1,512,256]{2,1,0:T(8,128)(2,1)S(1)}, bf16[1,512,256]{2,1,0:T(8,128)(2,1)S(1)}, u32[]{:S(2)}, u32[]{:S(2)}) collective-permute-start(bf16[1,512,256]{2,1,0:T(8,128)(2,1)S(1)} %shard_map.147), channel_id=1, source_target_pairs={{0,2},{1,7},{2,4},{3,1},{4,6},{5,3},{6,0},{7,5},{8,10},{9,15},{10,... | collective-permute-start | bytes 786440 | tf_op jit(solution)/shard_map/ppermute | solution.py:52
  101.7 2.9 %collective-permute-start.29 = (f32[256,128]{1,0:T(8,128)S(1)}, f32[256,128]{1,0:T(8,128)S(1)}, u32[]{:S(2)}, u32[]{:S(2)}) collective-permute-start(f32[256,128]{1,0:T(8,128)S(1)} %add.401), channel_id=1, source_target_pairs={{0,64},{32,96},{64,0},{96,32},{128,192},{160,224},{192,128},{224,1... | collective-permute-start | bytes 393224 | tf_op jit(solution)/shard_map/ppermute | solution.py:452
  104.6 2.4 %collective-permute-done.29 = f32[256,128]{1,0:T(8,128)S(1)} collective-permute-done((f32[256,128]{1,0:T(8,128)S(1)}, f32[256,128]{1,0:T(8,128)S(1)}, u32[]{:S(2)}, u32[]{:S(2)}) %collective-permute-start.29) | collective-permute-done | bytes 131104 | tf_op jit(solution)/shard_map/ppermute | solution.py:452
  107.0 1.2 collective-permute-done.28.refs_1_
  108.3 0.7 collective-permute-start.30
  108.9 2.3 %collective-permute-done.30.refs_2_ = bf16[4,512,256]{2,1,0:T(8,128)(2,1)S(1)} collective-permute-done((bf16[4,512,256]{2,1,0:T(8,128)(2,1)S(1)}, bf16[4,512,256]{2,1,0:T(8,128)(2,1)S(1)}, u32[]{:S(2)}, u32[]{:S(2)}) %collective-permute-start.30) | collective-permute-done | bytes 1048608 | tf_op jit(solution)/shard_map/ppermute | solution.py:52
  111.5 1.9 %collective-permute-start.31 = (bf16[2,512,256]{2,1,0:T(8,128)(2,1)S(1)}, bf16[2,512,256]{2,1,0:T(8,128)(2,1)S(1)}, u32[]{:S(2)}, u32[]{:S(2)}) collective-permute-start(bf16[2,512,256]{2,1,0:T(8,128)(2,1)S(1)} %shard_map.149), channel_id=1, source_target_pairs={{0,8},{1,25},{2,10},{3,27},{4,12},{5,29},{6,14},{7,31},{8,16},{9,1... | collective-permute-start | bytes 1572872 | tf_op jit(solution)/shard_map/ppermute | solution.py:52
  113.4 3.5 %collective-permute-start.32 = (bf16[2,512,256]{2,1,0:T(8,128)(2,1)S(1)}, bf16[2,512,256]{2,1,0:T(8,128)(2,1)S(1)}, u32[]{:S(2)}, u32[]{:S(2)}) collective-permute-start(bf16[2,512,256]{2,1,0:T(8,128)(2,1)S(1)} %shard_map.148), channel_id=1, source_target_pairs={{0,2},{1,7},{2,4},{3,1},{4,6},{5,3},{6,0},{7,5},{8,10},{9,15},{10,... | collective-permute-start | bytes 1572872 | tf_op jit(solution)/shard_map/ppermute | solution.py:52
  117.0 3.0 %collective-permute-done.31.refs_1_ = bf16[2,512,256]{2,1,0:T(8,128)(2,1)S(1)} collective-permute-done((bf16[2,512,256]{2,1,0:T(8,128)(2,1)S(1)}, bf16[2,512,256]{2,1,0:T(8,128)(2,1)S(1)}, u32[]{:S(2)}, u32[]{:S(2)}) %collective-permute-start.31) | collective-permute-done | bytes 524320 | tf_op jit(solution)/shard_map/ppermute | solution.py:52
  119.9 8.1 %collective-permute-done.32.p1 = bf16[2,512,256]{2,1,0:T(8,128)(2,1)S(1)} collective-permute-done((bf16[2,512,256]{2,1,0:T(8,128)(2,1)S(1)}, bf16[2,512,256]{2,1,0:T(8,128)(2,1)S(1)}, u32[]{:S(2)}, u32[]{:S(2)}) %collective-permute-start.32) | collective-permute-done | bytes 524320 | tf_op jit(solution)/shard_map/ppermute | solution.py:52
  128.0 0.5 collective-permute-start.34
  128.5 1.2 shard_map.151
  130.0 0.7 collective-permute-done.34.p2
  130.7 1.7 %shard_map.152 = (f32[256,512]{1,0:T(8,128)}, f32[256,512]{1,0:T(8,128)}, f32[256,512]{1,0:T(8,128)}) custom-call(s32[1]{0:T(128)S(6)} %copy.14.g_ref, f32[1,512,256]{2,1,0:T(8,128)S(1)} %shard_map.150.p0, bf16[2,512,256]{2,1,0:T(8,128)(2,1)S(1)} %collective-permute-done.32.p1, bf16[2,512,256]{2,1,0:T(8,128)(2,1)S(1)} %collective-permute-done.34.p2, ...), custom_call_target="tpu_custom_call" | custom-call | bytes 4980736 | tf_op jit(solution)/shard_map/pallas_call | solution.py:402
  (64 shorter events, 2.9 us)
Async XLA Ops:
  0.7 1.0 copy-start.1
  1.8 0.7 copy-start.9
  3.2 4.5 %collective-permute-start = (bf16[528,256]{1,0:T(8,128)(2,1)S(1)}, bf16[528,256]{1,0:T(8,128)(2,1)S(1)}, u32[]{:S(2)}, u32[]{:S(2)}) collective-permute-start(bf16[528,256]{1,0:T(8,128)(2,1)S(1)} %shard_map.128.refs_0_.refs_1_), channel_id=1, source_target_pairs={{0,1},{1,0},{2,3},{3,2},{4,5},{5,4},{6,7},{7,6},{8,9},{9,8},{10,11... | collective-permute-start | bytes 811016 | tf_op jit(solution)/shard_map/ppermute | solution.py:52
  7.8 9.6 %collective-permute-start.1 = (bf16[2,528,256]{2,1,0:T(8,128)(2,1)S(1)}, bf16[2,528,256]{2,1,0:T(8,128)(2,1)S(1)}, u32[]{:S(2)}, u32[]{:S(2)}) collective-permute-start(bf16[2,528,256]{2,1,0:T(8,128)(2,1)S(1)} %shard_map.129), channel_id=1, source_target_pairs={{0,24},{1,9},{2,26},{3,11},{4,28},{5,13},{6,30},{7,15},{8,0},{9,17... | collective-permute-start | bytes 1622024 | tf_op jit(solution)/shard_map/ppermute | solution.py:52
  7.9 14.2 %collective-permute-start.2 = (bf16[2,528,256]{2,1,0:T(8,128)(2,1)S(1)}, bf16[2,528,256]{2,1,0:T(8,128)(2,1)S(1)}, u32[]{:S(2)}, u32[]{:S(2)}) collective-permute-start(bf16[2,528,256]{2,1,0:T(8,128)(2,1)S(1)} %shard_map.129), channel_id=1, source_target_pairs={{0,6},{1,3},{2,0},{3,5},{4,2},{5,7},{6,4},{7,1},{8,14},{9,11},{10,... | collective-permute-start | bytes 1622024 | tf_op jit(solution)/shard_map/ppermute | solution.py:52
  10.5 3.4 %copy-start = (bf16[1,512,8192]{2,1,0:T(8,128)(2,1)S(1)}, bf16[1,512,8192]{2,1,0:T(8,128)(2,1)}, u32[]{:S(2)}) copy-start(bf16[1,512,8192]{2,1,0:T(8,128)(2,1)} %param.9) | copy-start | bytes 25165828
  13.9 4.3 %copy-start.2 = (f32[1,256,512]{2,1,0:T(8,128)S(1)}, f32[1,256,512]{2,1,0:T(8,128)}, u32[]{:S(2)}) copy-start(f32[1,256,512]{2,1,0:T(8,128)} %param.12) | copy-start | bytes 1572868
  13.9 4.3 %copy-start.3 = (f32[256,512]{1,0:T(8,128)S(1)}, f32[256,512]{1,0:T(8,128)}, u32[]{:S(2)}) copy-start(f32[256,512]{1,0:T(8,128)} %o_ref.3) | copy-start | bytes 1572868
  17.4 6.7 %collective-permute-start.3 = (bf16[528,256]{1,0:T(8,128)(2,1)S(1)}, bf16[528,256]{1,0:T(8,128)(2,1)S(1)}, u32[]{:S(2)}, u32[]{:S(2)}) collective-permute-start(bf16[528,256]{1,0:T(8,128)(2,1)S(1)} %slice_bitcast_fusion), channel_id=1, source_target_pairs={{0,24},{1,9},{2,26},{3,11},{4,28},{5,13},{6,30},{7,15},{8,0},{9,17... | collective-permute-start | bytes 811016 | tf_op jit(solution)/shard_map/ppermute | solution.py:52
  18.3 32.6 %copy-start.4 = (bf16[1,512,512]{2,1,0:T(8,128)(2,1)S(1)}, bf16[1,512,512]{2,1,0:T(8,128)(2,1)}, u32[]{:S(2)}) copy-start(bf16[1,512,512]{2,1,0:T(8,128)(2,1)} %param.11) | copy-start | bytes 1572868
  24.2 5.6 %collective-permute-start.5 = (bf16[2,528,256]{2,1,0:T(8,128)(2,1)S(1)}, bf16[2,528,256]{2,1,0:T(8,128)(2,1)S(1)}, u32[]{:S(2)}, u32[]{:S(2)}) collective-permute-start(bf16[2,528,256]{2,1,0:T(8,128)(2,1)S(1)} %collective-permute-done.2.refs_2_.refs_3_), channel_id=1, source_target_pairs={{0,1},{1,0},{2,3},{3,2},{4,5},{5,4},{6,7},{7,6},{8,9},{9,8},{10,11... | collective-permute-start | bytes 1622024 | tf_op jit(solution)/shard_map/ppermute | solution.py:52
  29.8 15.7 %collective-permute-start.10 = (bf16[4,512,256]{2,1,0:T(8,128)(2,1)S(1)}, bf16[4,512,256]{2,1,0:T(8,128)(2,1)S(1)}, u32[]{:S(2)}, u32[]{:S(2)}) collective-permute-start(bf16[4,512,256]{2,1,0:T(8,128)(2,1)S(1)} %get-tuple-element.87), channel_id=1, source_target_pairs={{0,1},{1,0},{2,3},{3,2},{4,5},{5,4},{6,7},{7,6},{8,9},{9,8},{10,11... | collective-permute-start | bytes 3145736 | tf_op jit(solution)/shard_map/ppermute | solution.py:52
  30.2 15.4 %collective-permute-start.9 = (bf16[4,512,256]{2,1,0:T(8,128)(2,1)S(1)}, bf16[4,512,256]{2,1,0:T(8,128)(2,1)S(1)}, u32[]{:S(2)}, u32[]{:S(2)}) collective-permute-start(bf16[4,512,256]{2,1,0:T(8,128)(2,1)S(1)} %get-tuple-element.85), channel_id=1, source_target_pairs={{0,1},{1,0},{2,3},{3,2},{4,5},{5,4},{6,7},{7,6},{8,9},{9,8},{10,11... | collective-permute-start | bytes 3145736 | tf_op jit(solution)/shard_map/ppermute | solution.py:52
  30.3 11.1 %collective-permute-start.4 = (bf16[2,528,256]{2,1,0:T(8,128)(2,1)S(1)}, bf16[2,528,256]{2,1,0:T(8,128)(2,1)S(1)}, u32[]{:S(2)}, u32[]{:S(2)}) collective-permute-start(bf16[2,528,256]{2,1,0:T(8,128)(2,1)S(1)} %collective-permute-done.2.refs_2_.refs_3_), channel_id=1, source_target_pairs={{0,24},{1,9},{2,26},{3,11},{4,28},{5,13},{6,30},{7,15},{8,0},{9,17... | collective-permute-start | bytes 1622024 | tf_op jit(solution)/shard_map/ppermute | solution.py:52
  30.4 11.1 %collective-permute-start.7 = (bf16[528,256]{1,0:T(8,128)(2,1)S(1)}, bf16[528,256]{1,0:T(8,128)(2,1)S(1)}, u32[]{:S(2)}, u32[]{:S(2)}) collective-permute-start(bf16[528,256]{1,0:T(8,128)(2,1)S(1)} %slice_bitcast_fusion.2), channel_id=1, source_target_pairs={{0,6},{1,3},{2,0},{3,5},{4,2},{5,7},{6,4},{7,1},{8,14},{9,11},{10,... | collective-permute-start | bytes 811016 | tf_op jit(solution)/shard_map/ppermute | solution.py:52
  32.0 13.5 %collective-permute-start.6 = (bf16[2,528,256]{2,1,0:T(8,128)(2,1)S(1)}, bf16[2,528,256]{2,1,0:T(8,128)(2,1)S(1)}, u32[]{:S(2)}, u32[]{:S(2)}) collective-permute-start(bf16[2,528,256]{2,1,0:T(8,128)(2,1)S(1)} %collective-permute-done.5), channel_id=1, source_target_pairs={{0,24},{1,9},{2,26},{3,11},{4,28},{5,13},{6,30},{7,15},{8,0},{9,17... | collective-permute-start | bytes 1622024 | tf_op jit(solution)/shard_map/ppermute | solution.py:52
  41.5 2.6 %collective-permute-start.8 = (bf16[528,256]{1,0:T(8,128)(2,1)S(1)}, bf16[528,256]{1,0:T(8,128)(2,1)S(1)}, u32[]{:S(2)}, u32[]{:S(2)}) collective-permute-start(bf16[528,256]{1,0:T(8,128)(2,1)S(1)} %collective-permute-done.7.refs_0_.refs_2_.refs_6_), channel_id=1, source_target_pairs={{0,1},{1,0},{2,3},{3,2},{4,5},{5,4},{6,7},{7,6},{8,9},{9,8},{10,11... | collective-permute-start | bytes 811016 | tf_op jit(solution)/shard_map/ppermute | solution.py:52
  45.6 7.7 %collective-permute-start.14 = (bf16[4,512,256]{2,1,0:T(8,128)(2,1)S(1)}, bf16[4,512,256]{2,1,0:T(8,128)(2,1)S(1)}, u32[]{:S(2)}, u32[]{:S(2)}) collective-permute-start(bf16[4,512,256]{2,1,0:T(8,128)(2,1)S(1)} %get-tuple-element.97), channel_id=1, source_target_pairs={{0,1},{1,0},{2,3},{3,2},{4,5},{5,4},{6,7},{7,6},{8,9},{9,8},{10,11... | collective-permute-start | bytes 3145736 | tf_op jit(solution)/shard_map/ppermute | solution.py:52
  45.9 16.3 %collective-permute-start.11 = (bf16[4,512,256]{2,1,0:T(8,128)(2,1)S(1)}, bf16[4,512,256]{2,1,0:T(8,128)(2,1)S(1)}, u32[]{:S(2)}, u32[]{:S(2)}) collective-permute-start(bf16[4,512,256]{2,1,0:T(8,128)(2,1)S(1)} %get-tuple-element.91), channel_id=1, source_target_pairs={{0,1},{1,0},{2,3},{3,2},{4,5},{5,4},{6,7},{7,6},{8,9},{9,8},{10,11... | collective-permute-start | bytes 3145736 | tf_op jit(solution)/shard_map/ppermute | solution.py:52
  46.1 4.8 %collective-permute-start.17 = (f32[256,128]{1,0:T(8,128)S(1)}, f32[256,128]{1,0:T(8,128)S(1)}, u32[]{:S(2)}, u32[]{:S(2)}) collective-permute-start(f32[256,128]{1,0:T(8,128)S(1)} %shard_map.131), channel_id=1, source_target_pairs={{0,128},{32,160},{64,192},{96,224},{128,0},{160,32},{192,64},{224,... | collective-permute-start | bytes 393224 | tf_op jit(solution)/shard_map/ppermute | solution.py:452
  46.7 9.6 %collective-permute-start.13 = (bf16[2,528,256]{2,1,0:T(8,128)(2,1)S(1)}, bf16[2,528,256]{2,1,0:T(8,128)(2,1)S(1)}, u32[]{:S(2)}, u32[]{:S(2)}) collective-permute-start(bf16[2,528,256]{2,1,0:T(8,128)(2,1)S(1)} %shard_map.133), channel_id=1, source_target_pairs={{0,24},{1,9},{2,26},{3,11},{4,28},{5,13},{6,30},{7,15},{8,0},{9,17... | collective-permute-start | bytes 1622024 | tf_op jit(solution)/shard_map/ppermute | solution.py:52
  46.8 15.3 %collective-permute-start.12 = (bf16[2,528,256]{2,1,0:T(8,128)(2,1)S(1)}, bf16[2,528,256]{2,1,0:T(8,128)(2,1)S(1)}, u32[]{:S(2)}, u32[]{:S(2)}) collective-permute-start(bf16[2,528,256]{2,1,0:T(8,128)(2,1)S(1)} %shard_map.132), channel_id=1, source_target_pairs={{0,24},{1,9},{2,26},{3,11},{4,28},{5,13},{6,30},{7,15},{8,0},{9,17... | collective-permute-start | bytes 1622024 | tf_op jit(solution)/shard_map/ppermute | solution.py:52
  47.6 5.7 %copy-start.10 = (s32[1,512]{1,0:T(1,128)S(1)}, s32[1,512]{1,0:T(1,128)}, u32[]{:S(2)}) copy-start(s32[1,512]{1,0:T(1,128)} %i_ref.3) | copy-start | bytes 6148
  50.9 4.4 %collective-permute-start.16 = (bf16[512,512]{1,0:T(8,128)(2,1)S(1)}, bf16[512,512]{1,0:T(8,128)(2,1)S(1)}, u32[]{:S(2)}, u32[]{:S(2)}) collective-permute-start(bf16[512,512]{1,0:T(8,128)(2,1)S(1)} %bitcast.52), channel_id=1, source_target_pairs={{0,1},{1,0},{2,3},{3,2},{4,5},{5,4},{6,7},{7,6},{8,9},{9,8},{10,11... | collective-permute-start | bytes 1572872 | tf_op jit(solution)/shard_map/ppermute | solution.py:52
  53.3 2.0 %collective-permute-start.15 = (s32[1,512]{1,0:T(1,128)S(1)}, s32[1,512]{1,0:T(1,128)S(1)}, u32[]{:S(2)}, u32[]{:S(2)}) collective-permute-start(s32[1,512]{1,0:T(1,128)S(1)} %copy-done.10), channel_id=1, source_target_pairs={{0,1},{1,0},{2,3},{3,2},{4,5},{5,4},{6,7},{7,6},{8,9},{9,8},{10,11... | collective-permute-start | bytes 6152 | tf_op jit(solution)/shard_map/ppermute | solution.py:52
  62.1 6.6 %collective-permute-start.18 = (bf16[528,256]{1,0:T(8,128)(2,1)S(1)}, bf16[528,256]{1,0:T(8,128)(2,1)S(1)}, u32[]{:S(2)}, u32[]{:S(2)}) collective-permute-start(bf16[528,256]{1,0:T(8,128)(2,1)S(1)} %slice_bitcast_fusion.1), channel_id=1, source_target_pairs={{0,24},{1,9},{2,26},{3,11},{4,28},{5,13},{6,30},{7,15},{8,0},{9,17... | collective-permute-start | bytes 811016 | tf_op jit(solution)/shard_map/ppermute | solution.py:52
  68.8 3.2 %collective-permute-start.19 = (f32[8,256]{1,0:T(8,128)S(1)}, f32[8,256]{1,0:T(8,128)S(1)}, u32[]{:S(2)}, u32[]{:S(2)}) collective-permute-start(f32[8,256]{1,0:T(8,128)S(1)} %shard_map.137.n_ref), channel_id=1, source_target_pairs={{0,1},{1,0},{2,3},{3,2},{4,5},{5,4},{6,7},{7,6},{8,9},{9,8},{10,11... | collective-permute-start | bytes 24584 | tf_op jit(solution)/shard_map/ppermute | solution.py:52
  71.9 2.7 %collective-permute-start.20 = (bf16[512,1024]{1,0:T(8,128)(2,1)S(1)}, bf16[512,1024]{1,0:T(8,128)(2,1)S(1)}, u32[]{:S(2)}, u32[]{:S(2)}) collective-permute-start(bf16[512,1024]{1,0:T(8,128)(2,1)S(1)} %get-tuple-element.112), channel_id=1, source_target_pairs={{0,1},{1,0},{2,3},{3,2},{4,5},{5,4},{6,7},{7,6},{8,9},{9,8},{10,11... | collective-permute-start | bytes 3145736 | tf_op jit(solution)/shard_map/ppermute | solution.py:52
  75.2 6.8 %collective-permute-start.21 = (bf16[1,512,256]{2,1,0:T(8,128)(2,1)S(1)}, bf16[1,512,256]{2,1,0:T(8,128)(2,1)S(1)}, u32[]{:S(2)}, u32[]{:S(2)}) collective-permute-start(bf16[1,512,256]{2,1,0:T(8,128)(2,1)S(1)} %get-tuple-element.117), channel_id=1, source_target_pairs={{0,8},{1,25},{2,10},{3,27},{4,12},{5,29},{6,14},{7,31},{8,16},{9,1... | collective-permute-start | bytes 786440 | tf_op jit(solution)/shard_map/ppermute | solution.py:52
  80.2 8.4 %collective-permute-start.22 = (bf16[2,512,256]{2,1,0:T(8,128)(2,1)S(1)}, bf16[2,512,256]{2,1,0:T(8,128)(2,1)S(1)}, u32[]{:S(2)}, u32[]{:S(2)}) collective-permute-start(bf16[2,512,256]{2,1,0:T(8,128)(2,1)S(1)} %get-tuple-element.121), channel_id=1, source_target_pairs={{0,8},{1,25},{2,10},{3,27},{4,12},{5,29},{6,14},{7,31},{8,16},{9,1... | collective-permute-start | bytes 1572872 | tf_op jit(solution)/shard_map/ppermute | solution.py:52
  80.3 5.2 %collective-permute-start.23 = (f32[256,128]{1,0:T(8,128)S(1)}, f32[256,128]{1,0:T(8,128)S(1)}, u32[]{:S(2)}, u32[]{:S(2)}) collective-permute-start(f32[256,128]{1,0:T(8,128)S(1)} %add.400), channel_id=1, source_target_pairs={{0,32},{32,0},{64,96},{96,64},{128,160},{160,128},{192,224},{224,1... | collective-permute-start | bytes 393224 | tf_op jit(solution)/shard_map/ppermute | solution.py:452
  82.0 12.2 %collective-permute-start.25 = (bf16[2,512,256]{2,1,0:T(8,128)(2,1)S(1)}, bf16[2,512,256]{2,1,0:T(8,128)(2,1)S(1)}, u32[]{:S(2)}, u32[]{:S(2)}) collective-permute-start(bf16[2,512,256]{2,1,0:T(8,128)(2,1)S(1)} %shard_map.143), channel_id=1, source_target_pairs={{0,8},{1,25},{2,10},{3,27},{4,12},{5,29},{6,14},{7,31},{8,16},{9,1... | collective-permute-start | bytes 1572872 | tf_op jit(solution)/shard_map/ppermute | solution.py:52
  88.8 19.5 %collective-permute-start.24 = (bf16[4,512,256]{2,1,0:T(8,128)(2,1)S(1)}, bf16[4,512,256]{2,1,0:T(8,128)(2,1)S(1)}, u32[]{:S(2)}, u32[]{:S(2)}) collective-permute-start(bf16[4,512,256]{2,1,0:T(8,128)(2,1)S(1)} %shard_map.145), channel_id=1, source_target_pairs={{0,8},{1,25},{2,10},{3,27},{4,12},{5,29},{6,14},{7,31},{8,16},{9,1... | collective-permute-start | bytes 3145736 | tf_op jit(solution)/shard_map/ppermute | solution.py:52
  94.2 3.8 %collective-permute-start.26 = (bf16[2,512,256]{2,1,0:T(8,128)(2,1)S(1)}, bf16[2,512,256]{2,1,0:T(8,128)(2,1)S(1)}, u32[]{:S(2)}, u32[]{:S(2)}) collective-permute-start(bf16[2,512,256]{2,1,0:T(8,128)(2,1)S(1)} %collective-permute-done.25.refs_1_), channel_id=1, source_target_pairs={{0,1},{1,0},{2,3},{3,2},{4,5},{5,4},{6,7},{7,6},{8,9},{9,8},{10,11... | collective-permute-start | bytes 1572872 | tf_op jit(solution)/shard_map/ppermute | solution.py:52
  96.1 12.1 %collective-permute-start.28 = (bf16[1,512,256]{2,1,0:T(8,128)(2,1)S(1)}, bf16[1,512,256]{2,1,0:T(8,128)(2,1)S(1)}, u32[]{:S(2)}, u32[]{:S(2)}) collective-permute-start(bf16[1,512,256]{2,1,0:T(8,128)(2,1)S(1)} %get-tuple-element.128), channel_id=1, source_target_pairs={{0,8},{1,25},{2,10},{3,27},{4,12},{5,29},{6,14},{7,31},{8,16},{9,1... | collective-permute-start | bytes 786440 | tf_op jit(solution)/shard_map/ppermute | solution.py:52
  98.1 10.2 %collective-permute-start.27 = (bf16[1,512,256]{2,1,0:T(8,128)(2,1)S(1)}, bf16[1,512,256]{2,1,0:T(8,128)(2,1)S(1)}, u32[]{:S(2)}, u32[]{:S(2)}) collective-permute-start(bf16[1,512,256]{2,1,0:T(8,128)(2,1)S(1)} %shard_map.147), channel_id=1, source_target_pairs={{0,2},{1,7},{2,4},{3,1},{4,6},{5,3},{6,0},{7,5},{8,10},{9,15},{10,... | collective-permute-start | bytes 786440 | tf_op jit(solution)/shard_map/ppermute | solution.py:52
  101.7 5.3 %collective-permute-start.29 = (f32[256,128]{1,0:T(8,128)S(1)}, f32[256,128]{1,0:T(8,128)S(1)}, u32[]{:S(2)}, u32[]{:S(2)}) collective-permute-start(f32[256,128]{1,0:T(8,128)S(1)} %add.401), channel_id=1, source_target_pairs={{0,64},{32,96},{64,0},{96,32},{128,192},{160,224},{192,128},{224,1... | collective-permute-start | bytes 393224 | tf_op jit(solution)/shard_map/ppermute | solution.py:452
  108.3 2.9 %collective-permute-start.30 = (bf16[4,512,256]{2,1,0:T(8,128)(2,1)S(1)}, bf16[4,512,256]{2,1,0:T(8,128)(2,1)S(1)}, u32[]{:S(2)}, u32[]{:S(2)}) collective-permute-start(bf16[4,512,256]{2,1,0:T(8,128)(2,1)S(1)} %collective-permute-done.24.refs_1_), channel_id=1, source_target_pairs={{0,1},{1,0},{2,3},{3,2},{4,5},{5,4},{6,7},{7,6},{8,9},{9,8},{10,11... | collective-permute-start | bytes 3145736 | tf_op jit(solution)/shard_map/ppermute | solution.py:52
  111.4 17.1 %copy-start.5 = (f32[256,512]{1,0:T(8,128)S(1)}, f32[256,512]{1,0:T(8,128)}, u32[]{:S(2)}) copy-start(f32[256,512]{1,0:T(8,128)} %m_ref.1) | copy-start | bytes 1572868
  111.5 19.1 %copy-start.6 = (f32[1,256,512]{2,1,0:T(8,128)S(1)}, f32[1,256,512]{2,1,0:T(8,128)}, u32[]{:S(2)}) copy-start(f32[1,256,512]{2,1,0:T(8,128)} %param.13) | copy-start | bytes 1572868
  111.5 19.1 %copy-start.7 = (f32[1,256,512]{2,1,0:T(8,128)S(1)}, f32[1,256,512]{2,1,0:T(8,128)}, u32[]{:S(2)}) copy-start(f32[1,256,512]{2,1,0:T(8,128)} %param.14) | copy-start | bytes 1572868
  111.5 8.4 %collective-permute-start.31 = (bf16[2,512,256]{2,1,0:T(8,128)(2,1)S(1)}, bf16[2,512,256]{2,1,0:T(8,128)(2,1)S(1)}, u32[]{:S(2)}, u32[]{:S(2)}) collective-permute-start(bf16[2,512,256]{2,1,0:T(8,128)(2,1)S(1)} %shard_map.149), channel_id=1, source_target_pairs={{0,8},{1,25},{2,10},{3,27},{4,12},{5,29},{6,14},{7,31},{8,16},{9,1... | collective-permute-start | bytes 1572872 | tf_op jit(solution)/shard_map/ppermute | solution.py:52
  113.4 14.6 %collective-permute-start.32 = (bf16[2,512,256]{2,1,0:T(8,128)(2,1)S(1)}, bf16[2,512,256]{2,1,0:T(8,128)(2,1)S(1)}, u32[]{:S(2)}, u32[]{:S(2)}) collective-permute-start(bf16[2,512,256]{2,1,0:T(8,128)(2,1)S(1)} %shard_map.148), channel_id=1, source_target_pairs={{0,2},{1,7},{2,4},{3,1},{4,6},{5,3},{6,0},{7,5},{8,10},{9,15},{10,... | collective-permute-start | bytes 1572872 | tf_op jit(solution)/shard_map/ppermute | solution.py:52
  128.0 1.9 %collective-permute-start.33 = (bf16[2,512,256]{2,1,0:T(8,128)(2,1)S(1)}, bf16[2,512,256]{2,1,0:T(8,128)(2,1)S(1)}, u32[]{:S(2)}, u32[]{:S(2)}) collective-permute-start(bf16[2,512,256]{2,1,0:T(8,128)(2,1)S(1)} %collective-permute-done.31.refs_1_), channel_id=1, source_target_pairs={{0,1},{1,0},{2,3},{3,2},{4,5},{5,4},{6,7},{7,6},{8,9},{9,8},{10,11... | collective-permute-start | bytes 1572872 | tf_op jit(solution)/shard_map/ppermute | solution.py:52
  128.0 2.7 %collective-permute-start.34 = (bf16[2,512,256]{2,1,0:T(8,128)(2,1)S(1)}, bf16[2,512,256]{2,1,0:T(8,128)(2,1)S(1)}, u32[]{:S(2)}, u32[]{:S(2)}) collective-permute-start(bf16[2,512,256]{2,1,0:T(8,128)(2,1)S(1)} %collective-permute-done.32.p1), channel_id=1, source_target_pairs={{0,1},{1,0},{2,3},{3,2},{4,5},{5,4},{6,7},{7,6},{8,9},{9,8},{10,11... | collective-permute-start | bytes 1572872 | tf_op jit(solution)/shard_map/ppermute | solution.py:52
  129.6 1.0 copy-start.8

commit v2 on v1

--- a/solution.py
+++ b/solution.py
@@ -520,8 +520,7 @@
     g2, s1 = together(g2, s1)
     s3 = combine([[(0, 0), (1, 0), (2, 1)]], bf16, P2, g2, move(g2, SIBLING))
     u2 = move(s3, TO_Z)
-    summed = swapped(after(summed, s3), 2)
-    g1, u2, f0, summed = together(g1, u2, f0, summed)
+    g1, u2, f0 = together(g1, u2, f0)
     c1 = move(g1, SIBLING)
     s4 = combine(
         [[(0, 0), (1, 2), (2, 3), (3, 0)], [(0, 1), (1, 0), (2, 1)]], bf16, PN, g1, c1, u2
@@ -529,10 +528,9 @@
     h = move(s4, TO_Z)
     s0 = combine([[(0, 1), (1, 0)], [(0, 2)]], bf16, P0, after(f0, s4))
     g0 = move(s0, TO_X)
-    outer_out, moment_out = outer_step(
-        fragment, after(summed, s0), outer_weight, outer_moment, replicas
-    )
-    g0, h = together(g0, h)
+    summed = swapped(after(summed, s0), 2)
+    outer_out, moment_out = outer_step(fragment, summed, outer_weight, outer_moment, replicas)
+    g0, h, outer_out, moment_out = together(g0, h, outer_out, moment_out)
     mine = combine([[(0, 0), (1, 0), (2, 1)]], f32, P0, g0, move(g0, SIBLING))
     inner_out, first_out, second_out = inner_step(
         fragment, (mine, h, move(h, SIBLING)), weight, adam_first[0], adam_second[0], outer_out

time: 133 us -> 133 us (level)
  transfers between devices with their start and end apart: 35 -> 35, of which waited for: 24 -> 23; matrix products, arithmetic and copies ran while one was open for 1% -> 1% of each run, Pallas kernels for 11% -> 11%
where the time goes in v2:
time: 133 us; the launch traced here: 132 us
  waiting for transfers between devices  59.8 us (45%)
  starting transfers between devices  46 us (35%)
  Pallas kernels  18.3 us (14%)
  local copies, waits for them, and re-layouts  6.35 us (5%)
  between operations  1.63 us (1%)
    ppermute x32, waiting for transfers between devices, move(): return lax.ppermute(value, 'fsdp', table)  53.9 us
    ppermute x32, starting transfers between devices, move(): return lax.ppermute(value, 'fsdp', table)  41.2 us
    ppermute x3, waiting for transfers between devices, swapped(): lax.ppermute(value, 'replica', [(r, r ^ step) for r in range(replicas)])  5.97 us
    pallas_call x4, Pallas kernels, add_keys(): pl.pallas_call(body, in_specs=in_vmem(1 + p + m + len(extra)), out_specs=...  5.18 us
    unnamed x22, local copies, waits for them, and re-layouts  5.14 us
    ppermute x3, starting transfers between devices, swapped(): lax.ppermute(value, 'replica', [(r, r ^ step) for r in range(replicas)])  4.86 us
    pallas_call x3, Pallas kernels, grads(): pl.pallas_call(body, in_specs=in_vmem(2 + p), out_specs=in_vmem(len(piece...  4.62 us
  transfers between devices with their start and end apart: 35, of which 23 were waited for; matrix products, arithmetic and copies ran while one was open for 1% of the time, Pallas kernels for 11%

profile of v2, /device:TPU:1, one launch (start us, length us, event | category | flops | bytes accessed | tf_op | source)
XLA Modules:
  0.0 132.3 jit_solution(14301422167847189814)
XLA Ops:
  0.7 1.0 copy-done.1
  1.8 0.7 copy-done.9
  2.4 0.8 shard_map.128.refs_0_.refs_1_
  3.2 3.3 %collective-permute-start = (bf16[528,256]{1,0:T(8,128)(2,1)S(1)}, bf16[528,256]{1,0:T(8,128)(2,1)S(1)}, u32[]{:S(2)}, u32[]{:S(2)}) collective-permute-start(bf16[528,256]{1,0:T(8,128)(2,1)S(1)} %shard_map.128.refs_0_.refs_1_), channel_id=1, source_target_pairs={{0,1},{1,0},{2,3},{3,2},{4,5},{5,4},{6,7},{7,6},{8,9},{9,8},{10,11... | collective-permute-start | bytes 811016 | tf_op jit(solution)/shard_map/ppermute | solution.py:52
  6.6 1.2 collective-permute-done.refs_1_
  7.9 2.5 %collective-permute-start.2 = (bf16[2,528,256]{2,1,0:T(8,128)(2,1)S(1)}, bf16[2,528,256]{2,1,0:T(8,128)(2,1)S(1)}, u32[]{:S(2)}, u32[]{:S(2)}) collective-permute-start(bf16[2,528,256]{2,1,0:T(8,128)(2,1)S(1)} %shard_map.129), channel_id=1, source_target_pairs={{0,6},{1,3},{2,0},{3,5},{4,2},{5,7},{6,4},{7,1},{8,14},{9,11},{10,... | collective-permute-start | bytes 1622024 | tf_op jit(solution)/shard_map/ppermute | solution.py:52
  10.5 3.4 %copy-done = bf16[1,512,8192]{2,1,0:T(8,128)(2,1)S(1)} copy-done((bf16[1,512,8192]{2,1,0:T(8,128)(2,1)S(1)}, bf16[1,512,8192]{2,1,0:T(8,128)(2,1)}, u32[]{:S(2)}) %copy-start) | copy-done | bytes 8388632
  13.9 2.3 %shard_map.130 = (bf16[16,512,256]{2,1,0:T(8,128)(2,1)S(1)}, bf16[4,512,256]{2,1,0:T(8,128)(2,1)S(1)}, bf16[4,512,256]{2,1,0:T(8,128)(2,1)S(1)}, bf16[4,512,256]...) custom-call(s32[16]{0:T(128)S(1)} %stack.130.b_ref, s32[16]{0:T(128)S(1)} %stack.147.d_ref, bf16[512,8192]{1,0:T(8,128)(2,1)S(1)} %bitcast.48), custom_call_target="tpu_custom_call" | custom-call | bytes 16777216 | tf_op jit(solution)/shard_map/pallas_call | solution.py:194
  16.3 1.2 collective-permute-done.1.refs_2_.refs_1_
  18.3 3.8 %collective-permute-done.2.refs_2_.refs_3_ = bf16[2,528,256]{2,1,0:T(8,128)(2,1)S(1)} collective-permute-done((bf16[2,528,256]{2,1,0:T(8,128)(2,1)S(1)}, bf16[2,528,256]{2,1,0:T(8,128)(2,1)S(1)}, u32[]{:S(2)}, u32[]{:S(2)}) %collective-permute-start.2) | collective-permute-done | bytes 540704 | tf_op jit(solution)/shard_map/ppermute | solution.py:52
  22.1 2.1 %collective-permute-done.3.refs_3_.refs_2_ = bf16[528,256]{1,0:T(8,128)(2,1)S(1)} collective-permute-done((bf16[528,256]{1,0:T(8,128)(2,1)S(1)}, bf16[528,256]{1,0:T(8,128)(2,1)S(1)}, u32[]{:S(2)}, u32[]{:S(2)}) %collective-permute-start.3) | collective-permute-done | bytes 270368 | tf_op jit(solution)/shard_map/ppermute | solution.py:52
  24.2 4.1 %collective-permute-start.5 = (bf16[2,528,256]{2,1,0:T(8,128)(2,1)S(1)}, bf16[2,528,256]{2,1,0:T(8,128)(2,1)S(1)}, u32[]{:S(2)}, u32[]{:S(2)}) collective-permute-start(bf16[2,528,256]{2,1,0:T(8,128)(2,1)S(1)} %collective-permute-done.2.refs_2_.refs_3_), channel_id=1, source_target_pairs={{0,1},{1,0},{2,3},{3,2},{4,5},{5,4},{6,7},{7,6},{8,9},{9,8},{10,11... | collective-permute-start | bytes 1622024 | tf_op jit(solution)/shard_map/ppermute | solution.py:52
  28.3 1.6 %collective-permute-done.5 = bf16[2,528,256]{2,1,0:T(8,128)(2,1)S(1)} collective-permute-done((bf16[2,528,256]{2,1,0:T(8,128)(2,1)S(1)}, bf16[2,528,256]{2,1,0:T(8,128)(2,1)S(1)}, u32[]{:S(2)}, u32[]{:S(2)}) %collective-permute-start.5) | collective-permute-done | bytes 540704 | tf_op jit(solution)/shard_map/ppermute | solution.py:52
  29.8 0.4 collective-permute-start.10
  30.4 1.7 %collective-permute-start.7 = (bf16[528,256]{1,0:T(8,128)(2,1)S(1)}, bf16[528,256]{1,0:T(8,128)(2,1)S(1)}, u32[]{:S(2)}, u32[]{:S(2)}) collective-permute-start(bf16[528,256]{1,0:T(8,128)(2,1)S(1)} %slice_bitcast_fusion.2), channel_id=1, source_target_pairs={{0,6},{1,3},{2,0},{3,5},{4,2},{5,7},{6,4},{7,1},{8,14},{9,11},{10,... | collective-permute-start | bytes 811016 | tf_op jit(solution)/shard_map/ppermute | solution.py:52
  32.2 9.2 %collective-permute-done.7.refs_0_.refs_2_.refs_6_ = bf16[528,256]{1,0:T(8,128)(2,1)S(1)} collective-permute-done((bf16[528,256]{1,0:T(8,128)(2,1)S(1)}, bf16[528,256]{1,0:T(8,128)(2,1)S(1)}, u32[]{:S(2)}, u32[]{:S(2)}) %collective-permute-start.7) | collective-permute-done | bytes 270368 | tf_op jit(solution)/shard_map/ppermute | solution.py:52
  41.5 1.5 %collective-permute-start.8 = (bf16[528,256]{1,0:T(8,128)(2,1)S(1)}, bf16[528,256]{1,0:T(8,128)(2,1)S(1)}, u32[]{:S(2)}, u32[]{:S(2)}) collective-permute-start(bf16[528,256]{1,0:T(8,128)(2,1)S(1)} %collective-permute-done.7.refs_0_.refs_2_.refs_6_), channel_id=1, source_target_pairs={{0,1},{1,0},{2,3},{3,2},{4,5},{5,4},{6,7},{7,6},{8,9},{9,8},{10,11... | collective-permute-start | bytes 811016 | tf_op jit(solution)/shard_map/ppermute | solution.py:52
  42.9 1.2 collective-permute-done.8.refs_1_
  44.1 1.5 %collective-permute-done.6.refs_1_.refs_4_.refs_5_ = bf16[2,528,256]{2,1,0:T(8,128)(2,1)S(1)} collective-permute-done((bf16[2,528,256]{2,1,0:T(8,128)(2,1)S(1)}, bf16[2,528,256]{2,1,0:T(8,128)(2,1)S(1)}, u32[]{:S(2)}, u32[]{:S(2)}) %collective-permute-start.6) | collective-permute-done | bytes 540704 | tf_op jit(solution)/shard_map/ppermute | solution.py:52
  45.6 0.3 collective-permute-start.14
  46.1 0.6 collective-permute-start.17
  46.8 0.8 collective-permute-start.12
  47.6 3.3 %collective-permute-done.17 = f32[256,128]{1,0:T(8,128)S(1)} collective-permute-done((f32[256,128]{1,0:T(8,128)S(1)}, f32[256,128]{1,0:T(8,128)S(1)}, u32[]{:S(2)}, u32[]{:S(2)}) %collective-permute-start.17) | collective-permute-done | bytes 131104 | tf_op jit(solution)/shard_map/ppermute | solution.py:452
  50.9 1.1 collective-permute-start.16
  52.0 1.3 shard_map.134.refs_5_
  53.4 1.8 %shard_map.135.refs_5_ = f32[512,1024]{1,0:T(8,128)S(1)} custom-call(bf16[16,512,256]{2,1,0:T(8,128)(2,1)S(1)} %get-tuple-element.81.own_ref, bf16[4,512,256]{2,1,0:T(8,128)(2,1)S(1)} %collective-permute-done.10.refs_0_, bf16[4,512,256]{2,1,0:T(8,128)(2,1)S(1)} %collective-permute-done.14.refs_1_.refs_0_, ...), custom_call_target="tpu_custom_call" | custom-call | flops 1610612736 | bytes 2097152 | tf_op jit(solution)/shard_map/pallas_call | solution.py:244
  55.3 1.0 collective-permute-done.13.refs_4_.refs_8_
  56.3 5.8 %collective-permute-done.12.refs_3_.refs_7_ = bf16[2,528,256]{2,1,0:T(8,128)(2,1)S(1)} collective-permute-done((bf16[2,528,256]{2,1,0:T(8,128)(2,1)S(1)}, bf16[2,528,256]{2,1,0:T(8,128)(2,1)S(1)}, u32[]{:S(2)}, u32[]{:S(2)}) %collective-permute-start.12) | collective-permute-done | bytes 540704 | tf_op jit(solution)/shard_map/ppermute | solution.py:52
  62.2 1.6 %shard_map.136.refs_2_ = f32[512,1024]{1,0:T(8,128)S(1)} custom-call(bf16[16,512,256]{2,1,0:T(8,128)(2,1)S(1)} %get-tuple-element.81.own_ref, bf16[4,512,256]{2,1,0:T(8,128)(2,1)S(1)} %collective-permute-done.14.refs_1_.refs_0_, bf16[4,512,256]{2,1,0:T(8,128)(2,1)S(1)} %collective-permute-done.11.refs_1_.refs_0_, ...), custom_call_target="tpu_custom_call" | custom-call | flops 1342177280 | bytes 2097152 | tf_op jit(solution)/shard_map/pallas_call | solution.py:244
  63.8 4.9 %collective-permute-done.18.refs_9_.refs_1_ = bf16[528,256]{1,0:T(8,128)(2,1)S(1)} collective-permute-done((bf16[528,256]{1,0:T(8,128)(2,1)S(1)}, bf16[528,256]{1,0:T(8,128)(2,1)S(1)}, u32[]{:S(2)}, u32[]{:S(2)}) %collective-permute-start.18) | collective-permute-done | bytes 270368 | tf_op jit(solution)/shard_map/ppermute | solution.py:52
  68.8 2.3 %collective-permute-start.19 = (f32[8,256]{1,0:T(8,128)S(1)}, f32[8,256]{1,0:T(8,128)S(1)}, u32[]{:S(2)}, u32[]{:S(2)}) collective-permute-start(f32[8,256]{1,0:T(8,128)S(1)} %shard_map.137.n_ref), channel_id=1, source_target_pairs={{0,1},{1,0},{2,3},{3,2},{4,5},{5,4},{6,7},{7,6},{8,9},{9,8},{10,11... | collective-permute-start | bytes 24584 | tf_op jit(solution)/shard_map/ppermute | solution.py:52
  71.1 0.5 shard_map.138
  71.6 0.4 collective-permute-done.19.m_ref
  71.9 0.3 collective-permute-start.20
  72.3 0.6 shard_map.139
  72.9 1.0 fusion
  73.9 0.5 shard_map.140.refs_3_
  74.6 0.6 shard_map.141
  75.2 3.5 %collective-permute-start.21 = (bf16[1,512,256]{2,1,0:T(8,128)(2,1)S(1)}, bf16[1,512,256]{2,1,0:T(8,128)(2,1)S(1)}, u32[]{:S(2)}, u32[]{:S(2)}) collective-permute-start(bf16[1,512,256]{2,1,0:T(8,128)(2,1)S(1)} %get-tuple-element.117), channel_id=1, source_target_pairs={{0,8},{1,25},{2,10},{3,27},{4,12},{5,29},{6,14},{7,31},{8,16},{9,1... | collective-permute-start | bytes 786440 | tf_op jit(solution)/shard_map/ppermute | solution.py:52
  78.6 1.5 %shard_map.142 = (bf16[2,512,256]{2,1,0:T(8,128)(2,1)S(1)}, f32[3,512,256]{2,1,0:T(8,128)S(1)}) custom-call(bf16[16,512,256]{2,1,0:T(8,128)(2,1)S(1)} %get-tuple-element.81.own_ref, bf16[4,512,256]{2,1,0:T(8,128)(2,1)S(1)} %collective-permute-done.14.refs_1_.refs_0_, bf16[4,512,256]{2,1,0:T(8,128)(2,1)S(1)} %collective-permute-done.11.refs_1_.refs_0_, ...), custom_call_target="tpu_custom_call" | custom-call | flops 1342177280 | bytes 2621440 | tf_op jit(solution)/shard_map/pallas_call | solution.py:272
  80.3 1.4 %collective-permute-start.23 = (f32[256,128]{1,0:T(8,128)S(1)}, f32[256,128]{1,0:T(8,128)S(1)}, u32[]{:S(2)}, u32[]{:S(2)}) collective-permute-start(f32[256,128]{1,0:T(8,128)S(1)} %add.400), channel_id=1, source_target_pairs={{0,32},{32,0},{64,96},{96,64},{128,160},{160,128},{192,224},{224,1... | collective-permute-start | bytes 393224 | tf_op jit(solution)/shard_map/ppermute | solution.py:452
  81.7 0.3 collective-permute-done.21.refs_1_
  82.0 3.4 %collective-permute-start.25 = (bf16[2,512,256]{2,1,0:T(8,128)(2,1)S(1)}, bf16[2,512,256]{2,1,0:T(8,128)(2,1)S(1)}, u32[]{:S(2)}, u32[]{:S(2)}) collective-permute-start(bf16[2,512,256]{2,1,0:T(8,128)(2,1)S(1)} %shard_map.143), channel_id=1, source_target_pairs={{0,8},{1,25},{2,10},{3,27},{4,12},{5,29},{6,14},{7,31},{8,16},{9,1... | collective-permute-start | bytes 1572872 | tf_op jit(solution)/shard_map/ppermute | solution.py:52
  85.5 1.8 %shard_map.144 = (f32[2,512,256]{2,1,0:T(8,128)S(1)}, f32[4,512,256]{2,1,0:T(8,128)S(1)}) custom-call(bf16[16,512,256]{2,1,0:T(8,128)(2,1)S(1)} %get-tuple-element.81.own_ref, bf16[4,512,256]{2,1,0:T(8,128)(2,1)S(1)} %collective-permute-done.10.refs_0_, bf16[4,512,256]{2,1,0:T(8,128)(2,1)S(1)} %collective-permute-done.14.refs_1_.refs_0_, ...), custom_call_target="tpu_custom_call" | custom-call | flops 1610612736 | bytes 3145728 | tf_op jit(solution)/shard_map/pallas_call | solution.py:272
  87.3 1.3 collective-permute-done.22.refs_2_
  88.8 2.2 %collective-permute-start.24 = (bf16[4,512,256]{2,1,0:T(8,128)(2,1)S(1)}, bf16[4,512,256]{2,1,0:T(8,128)(2,1)S(1)}, u32[]{:S(2)}, u32[]{:S(2)}) collective-permute-start(bf16[4,512,256]{2,1,0:T(8,128)(2,1)S(1)} %shard_map.145), channel_id=1, source_target_pairs={{0,8},{1,25},{2,10},{3,27},{4,12},{5,29},{6,14},{7,31},{8,16},{9,1... | collective-permute-start | bytes 3145736 | tf_op jit(solution)/shard_map/ppermute | solution.py:52
  90.9 3.3 %collective-permute-done.25.refs_1_ = bf16[2,512,256]{2,1,0:T(8,128)(2,1)S(1)} collective-permute-done((bf16[2,512,256]{2,1,0:T(8,128)(2,1)S(1)}, bf16[2,512,256]{2,1,0:T(8,128)(2,1)S(1)}, u32[]{:S(2)}, u32[]{:S(2)}) %collective-permute-start.25) | collective-permute-done | bytes 524320 | tf_op jit(solution)/shard_map/ppermute | solution.py:52
  94.2 0.7 collective-permute-start.26
  94.9 1.3 shard_map.146
  96.1 1.8 %collective-permute-start.28 = (bf16[1,512,256]{2,1,0:T(8,128)(2,1)S(1)}, bf16[1,512,256]{2,1,0:T(8,128)(2,1)S(1)}, u32[]{:S(2)}, u32[]{:S(2)}) collective-permute-start(bf16[1,512,256]{2,1,0:T(8,128)(2,1)S(1)} %get-tuple-element.128), channel_id=1, source_target_pairs={{0,8},{1,25},{2,10},{3,27},{4,12},{5,29},{6,14},{7,31},{8,16},{9,1... | collective-permute-start | bytes 786440 | tf_op jit(solution)/shard_map/ppermute | solution.py:52
  98.1 3.6 %collective-permute-start.27 = (bf16[1,512,256]{2,1,0:T(8,128)(2,1)S(1)}, bf16[1,512,256]{2,1,0:T(8,128)(2,1)S(1)}, u32[]{:S(2)}, u32[]{:S(2)}) collective-permute-start(bf16[1,512,256]{2,1,0:T(8,128)(2,1)S(1)} %shard_map.147), channel_id=1, source_target_pairs={{0,2},{1,7},{2,4},{3,1},{4,6},{5,3},{6,0},{7,5},{8,10},{9,15},{10,... | collective-permute-start | bytes 786440 | tf_op jit(solution)/shard_map/ppermute | solution.py:52
  101.7 6.6 %collective-permute-done.28.refs_1_ = bf16[1,512,256]{2,1,0:T(8,128)(2,1)S(1)} collective-permute-done((bf16[1,512,256]{2,1,0:T(8,128)(2,1)S(1)}, bf16[1,512,256]{2,1,0:T(8,128)(2,1)S(1)}, u32[]{:S(2)}, u32[]{:S(2)}) %collective-permute-start.28) | collective-permute-done | bytes 262176 | tf_op jit(solution)/shard_map/ppermute | solution.py:52
  108.3 0.7 collective-permute-start.29
  108.9 2.3 %collective-permute-done.29.refs_2_ = bf16[4,512,256]{2,1,0:T(8,128)(2,1)S(1)} collective-permute-done((bf16[4,512,256]{2,1,0:T(8,128)(2,1)S(1)}, bf16[4,512,256]{2,1,0:T(8,128)(2,1)S(1)}, u32[]{:S(2)}, u32[]{:S(2)}) %collective-permute-start.29) | collective-permute-done | bytes 1048608 | tf_op jit(solution)/shard_map/ppermute | solution.py:52
  111.5 1.9 %collective-permute-start.30 = (bf16[2,512,256]{2,1,0:T(8,128)(2,1)S(1)}, bf16[2,512,256]{2,1,0:T(8,128)(2,1)S(1)}, u32[]{:S(2)}, u32[]{:S(2)}) collective-permute-start(bf16[2,512,256]{2,1,0:T(8,128)(2,1)S(1)} %shard_map.149), channel_id=1, source_target_pairs={{0,8},{1,25},{2,10},{3,27},{4,12},{5,29},{6,14},{7,31},{8,16},{9,1... | collective-permute-start | bytes 1572872 | tf_op jit(solution)/shard_map/ppermute | solution.py:52
  113.4 3.5 %collective-permute-start.31 = (bf16[2,512,256]{2,1,0:T(8,128)(2,1)S(1)}, bf16[2,512,256]{2,1,0:T(8,128)(2,1)S(1)}, u32[]{:S(2)}, u32[]{:S(2)}) collective-permute-start(bf16[2,512,256]{2,1,0:T(8,128)(2,1)S(1)} %shard_map.148), channel_id=1, source_target_pairs={{0,2},{1,7},{2,4},{3,1},{4,6},{5,3},{6,0},{7,5},{8,10},{9,15},{10,... | collective-permute-start | bytes 1572872 | tf_op jit(solution)/shard_map/ppermute | solution.py:52
  117.0 2.9 %collective-permute-start.32 = (f32[256,128]{1,0:T(8,128)S(1)}, f32[256,128]{1,0:T(8,128)S(1)}, u32[]{:S(2)}, u32[]{:S(2)}) collective-permute-start(f32[256,128]{1,0:T(8,128)S(1)} %add.401), channel_id=1, source_target_pairs={{0,64},{32,96},{64,0},{96,32},{128,192},{160,224},{192,128},{224,1... | collective-permute-start | bytes 393224 | tf_op jit(solution)/shard_map/ppermute | solution.py:452
  119.9 2.7 %collective-permute-done.32 = f32[256,128]{1,0:T(8,128)S(1)} collective-permute-done((f32[256,128]{1,0:T(8,128)S(1)}, f32[256,128]{1,0:T(8,128)S(1)}, u32[]{:S(2)}, u32[]{:S(2)}) %collective-permute-start.32) | collective-permute-done | bytes 131104 | tf_op jit(solution)/shard_map/ppermute | solution.py:452
  122.6 1.2 shard_map.150
  123.8 4.2 %collective-permute-done.31.p1 = bf16[2,512,256]{2,1,0:T(8,128)(2,1)S(1)} collective-permute-done((bf16[2,512,256]{2,1,0:T(8,128)(2,1)S(1)}, bf16[2,512,256]{2,1,0:T(8,128)(2,1)S(1)}, u32[]{:S(2)}, u32[]{:S(2)}) %collective-permute-start.31) | collective-permute-done | bytes 524320 | tf_op jit(solution)/shard_map/ppermute | solution.py:52
  128.0 0.5 collective-permute-start.34
  128.5 1.4 %collective-permute-done.33.refs_2_ = bf16[2,512,256]{2,1,0:T(8,128)(2,1)S(1)} collective-permute-done((bf16[2,512,256]{2,1,0:T(8,128)(2,1)S(1)}, bf16[2,512,256]{2,1,0:T(8,128)(2,1)S(1)}, u32[]{:S(2)}, u32[]{:S(2)}) %collective-permute-start.33) | collective-permute-done | bytes 524320 | tf_op jit(solution)/shard_map/ppermute | solution.py:52
  129.9 0.7 collective-permute-done.34.p2
  130.6 1.7 %shard_map.152 = (f32[256,512]{1,0:T(8,128)}, f32[256,512]{1,0:T(8,128)}, f32[256,512]{1,0:T(8,128)}) custom-call(s32[1]{0:T(128)S(6)} %copy.14.g_ref, f32[1,512,256]{2,1,0:T(8,128)S(1)} %shard_map.151.p0, bf16[2,512,256]{2,1,0:T(8,128)(2,1)S(1)} %collective-permute-done.31.p1, bf16[2,512,256]{2,1,0:T(8,128)(2,1)S(1)} %collective-permute-done.34.p2, ...), custom_call_target="tpu_custom_call" | custom-call | bytes 4980736 | tf_op jit(solution)/shard_map/pallas_call | solution.py:402
  (64 shorter events, 2.6 us)
Async XLA Ops:
  0.7 1.0 copy-start.1
  1.8 0.7 copy-start.9
  3.2 4.5 %collective-permute-start = (bf16[528,256]{1,0:T(8,128)(2,1)S(1)}, bf16[528,256]{1,0:T(8,128)(2,1)S(1)}, u32[]{:S(2)}, u32[]{:S(2)}) collective-permute-start(bf16[528,256]{1,0:T(8,128)(2,1)S(1)} %shard_map.128.refs_0_.refs_1_), channel_id=1, source_target_pairs={{0,1},{1,0},{2,3},{3,2},{4,5},{5,4},{6,7},{7,6},{8,9},{9,8},{10,11... | collective-permute-start | bytes 811016 | tf_op jit(solution)/shard_map/ppermute | solution.py:52
  7.8 9.6 %collective-permute-start.1 = (bf16[2,528,256]{2,1,0:T(8,128)(2,1)S(1)}, bf16[2,528,256]{2,1,0:T(8,128)(2,1)S(1)}, u32[]{:S(2)}, u32[]{:S(2)}) collective-permute-start(bf16[2,528,256]{2,1,0:T(8,128)(2,1)S(1)} %shard_map.129), channel_id=1, source_target_pairs={{0,24},{1,9},{2,26},{3,11},{4,28},{5,13},{6,30},{7,15},{8,0},{9,17... | collective-permute-start | bytes 1622024 | tf_op jit(solution)/shard_map/ppermute | solution.py:52
  7.9 14.2 %collective-permute-start.2 = (bf16[2,528,256]{2,1,0:T(8,128)(2,1)S(1)}, bf16[2,528,256]{2,1,0:T(8,128)(2,1)S(1)}, u32[]{:S(2)}, u32[]{:S(2)}) collective-permute-start(bf16[2,528,256]{2,1,0:T(8,128)(2,1)S(1)} %shard_map.129), channel_id=1, source_target_pairs={{0,6},{1,3},{2,0},{3,5},{4,2},{5,7},{6,4},{7,1},{8,14},{9,11},{10,... | collective-permute-start | bytes 1622024 | tf_op jit(solution)/shard_map/ppermute | solution.py:52
  10.5 3.4 %copy-start = (bf16[1,512,8192]{2,1,0:T(8,128)(2,1)S(1)}, bf16[1,512,8192]{2,1,0:T(8,128)(2,1)}, u32[]{:S(2)}) copy-start(bf16[1,512,8192]{2,1,0:T(8,128)(2,1)} %param.9) | copy-start | bytes 25165828
  13.9 4.3 %copy-start.2 = (f32[1,256,512]{2,1,0:T(8,128)S(1)}, f32[1,256,512]{2,1,0:T(8,128)}, u32[]{:S(2)}) copy-start(f32[1,256,512]{2,1,0:T(8,128)} %param.12) | copy-start | bytes 1572868
  13.9 4.3 %copy-start.3 = (f32[256,512]{1,0:T(8,128)S(1)}, f32[256,512]{1,0:T(8,128)}, u32[]{:S(2)}) copy-start(f32[256,512]{1,0:T(8,128)} %o_ref.3) | copy-start | bytes 1572868
  17.4 6.7 %collective-permute-start.3 = (bf16[528,256]{1,0:T(8,128)(2,1)S(1)}, bf16[528,256]{1,0:T(8,128)(2,1)S(1)}, u32[]{:S(2)}, u32[]{:S(2)}) collective-permute-start(bf16[528,256]{1,0:T(8,128)(2,1)S(1)} %slice_bitcast_fusion), channel_id=1, source_target_pairs={{0,24},{1,9},{2,26},{3,11},{4,28},{5,13},{6,30},{7,15},{8,0},{9,17... | collective-permute-start | bytes 811016 | tf_op jit(solution)/shard_map/ppermute | solution.py:52
  18.3 32.6 %copy-start.4 = (bf16[1,512,512]{2,1,0:T(8,128)(2,1)S(1)}, bf16[1,512,512]{2,1,0:T(8,128)(2,1)}, u32[]{:S(2)}) copy-start(bf16[1,512,512]{2,1,0:T(8,128)(2,1)} %param.11) | copy-start | bytes 1572868
  24.2 5.6 %collective-permute-start.5 = (bf16[2,528,256]{2,1,0:T(8,128)(2,1)S(1)}, bf16[2,528,256]{2,1,0:T(8,128)(2,1)S(1)}, u32[]{:S(2)}, u32[]{:S(2)}) collective-permute-start(bf16[2,528,256]{2,1,0:T(8,128)(2,1)S(1)} %collective-permute-done.2.refs_2_.refs_3_), channel_id=1, source_target_pairs={{0,1},{1,0},{2,3},{3,2},{4,5},{5,4},{6,7},{7,6},{8,9},{9,8},{10,11... | collective-permute-start | bytes 1622024 | tf_op jit(solution)/shard_map/ppermute | solution.py:52
  29.8 15.7 %collective-permute-start.10 = (bf16[4,512,256]{2,1,0:T(8,128)(2,1)S(1)}, bf16[4,512,256]{2,1,0:T(8,128)(2,1)S(1)}, u32[]{:S(2)}, u32[]{:S(2)}) collective-permute-start(bf16[4,512,256]{2,1,0:T(8,128)(2,1)S(1)} %get-tuple-element.87), channel_id=1, source_target_pairs={{0,1},{1,0},{2,3},{3,2},{4,5},{5,4},{6,7},{7,6},{8,9},{9,8},{10,11... | collective-permute-start | bytes 3145736 | tf_op jit(solution)/shard_map/ppermute | solution.py:52
  30.2 15.4 %collective-permute-start.9 = (bf16[4,512,256]{2,1,0:T(8,128)(2,1)S(1)}, bf16[4,512,256]{2,1,0:T(8,128)(2,1)S(1)}, u32[]{:S(2)}, u32[]{:S(2)}) collective-permute-start(bf16[4,512,256]{2,1,0:T(8,128)(2,1)S(1)} %get-tuple-element.85), channel_id=1, source_target_pairs={{0,1},{1,0},{2,3},{3,2},{4,5},{5,4},{6,7},{7,6},{8,9},{9,8},{10,11... | collective-permute-start | bytes 3145736 | tf_op jit(solution)/shard_map/ppermute | solution.py:52
  30.3 11.1 %collective-permute-start.4 = (bf16[2,528,256]{2,1,0:T(8,128)(2,1)S(1)}, bf16[2,528,256]{2,1,0:T(8,128)(2,1)S(1)}, u32[]{:S(2)}, u32[]{:S(2)}) collective-permute-start(bf16[2,528,256]{2,1,0:T(8,128)(2,1)S(1)} %collective-permute-done.2.refs_2_.refs_3_), channel_id=1, source_target_pairs={{0,24},{1,9},{2,26},{3,11},{4,28},{5,13},{6,30},{7,15},{8,0},{9,17... | collective-permute-start | bytes 1622024 | tf_op jit(solution)/shard_map/ppermute | solution.py:52
  30.4 11.1 %collective-permute-start.7 = (bf16[528,256]{1,0:T(8,128)(2,1)S(1)}, bf16[528,256]{1,0:T(8,128)(2,1)S(1)}, u32[]{:S(2)}, u32[]{:S(2)}) collective-permute-start(bf16[528,256]{1,0:T(8,128)(2,1)S(1)} %slice_bitcast_fusion.2), channel_id=1, source_target_pairs={{0,6},{1,3},{2,0},{3,5},{4,2},{5,7},{6,4},{7,1},{8,14},{9,11},{10,... | collective-permute-start | bytes 811016 | tf_op jit(solution)/shard_map/ppermute | solution.py:52
  32.0 13.5 %collective-permute-start.6 = (bf16[2,528,256]{2,1,0:T(8,128)(2,1)S(1)}, bf16[2,528,256]{2,1,0:T(8,128)(2,1)S(1)}, u32[]{:S(2)}, u32[]{:S(2)}) collective-permute-start(bf16[2,528,256]{2,1,0:T(8,128)(2,1)S(1)} %collective-permute-done.5), channel_id=1, source_target_pairs={{0,24},{1,9},{2,26},{3,11},{4,28},{5,13},{6,30},{7,15},{8,0},{9,17... | collective-permute-start | bytes 1622024 | tf_op jit(solution)/shard_map/ppermute | solution.py:52
  41.5 2.6 %collective-permute-start.8 = (bf16[528,256]{1,0:T(8,128)(2,1)S(1)}, bf16[528,256]{1,0:T(8,128)(2,1)S(1)}, u32[]{:S(2)}, u32[]{:S(2)}) collective-permute-start(bf16[528,256]{1,0:T(8,128)(2,1)S(1)} %collective-permute-done.7.refs_0_.refs_2_.refs_6_), channel_id=1, source_target_pairs={{0,1},{1,0},{2,3},{3,2},{4,5},{5,4},{6,7},{7,6},{8,9},{9,8},{10,11... | collective-permute-start | bytes 811016 | tf_op jit(solution)/shard_map/ppermute | solution.py:52
  45.6 7.7 %collective-permute-start.14 = (bf16[4,512,256]{2,1,0:T(8,128)(2,1)S(1)}, bf16[4,512,256]{2,1,0:T(8,128)(2,1)S(1)}, u32[]{:S(2)}, u32[]{:S(2)}) collective-permute-start(bf16[4,512,256]{2,1,0:T(8,128)(2,1)S(1)} %get-tuple-element.97), channel_id=1, source_target_pairs={{0,1},{1,0},{2,3},{3,2},{4,5},{5,4},{6,7},{7,6},{8,9},{9,8},{10,11... | collective-permute-start | bytes 3145736 | tf_op jit(solution)/shard_map/ppermute | solution.py:52
  45.9 16.3 %collective-permute-start.11 = (bf16[4,512,256]{2,1,0:T(8,128)(2,1)S(1)}, bf16[4,512,256]{2,1,0:T(8,128)(2,1)S(1)}, u32[]{:S(2)}, u32[]{:S(2)}) collective-permute-start(bf16[4,512,256]{2,1,0:T(8,128)(2,1)S(1)} %get-tuple-element.91), channel_id=1, source_target_pairs={{0,1},{1,0},{2,3},{3,2},{4,5},{5,4},{6,7},{7,6},{8,9},{9,8},{10,11... | collective-permute-start | bytes 3145736 | tf_op jit(solution)/shard_map/ppermute | solution.py:52
  46.1 4.8 %collective-permute-start.17 = (f32[256,128]{1,0:T(8,128)S(1)}, f32[256,128]{1,0:T(8,128)S(1)}, u32[]{:S(2)}, u32[]{:S(2)}) collective-permute-start(f32[256,128]{1,0:T(8,128)S(1)} %shard_map.131), channel_id=1, source_target_pairs={{0,128},{32,160},{64,192},{96,224},{128,0},{160,32},{192,64},{224,... | collective-permute-start | bytes 393224 | tf_op jit(solution)/shard_map/ppermute | solution.py:452
  46.7 9.6 %collective-permute-start.13 = (bf16[2,528,256]{2,1,0:T(8,128)(2,1)S(1)}, bf16[2,528,256]{2,1,0:T(8,128)(2,1)S(1)}, u32[]{:S(2)}, u32[]{:S(2)}) collective-permute-start(bf16[2,528,256]{2,1,0:T(8,128)(2,1)S(1)} %shard_map.133), channel_id=1, source_target_pairs={{0,24},{1,9},{2,26},{3,11},{4,28},{5,13},{6,30},{7,15},{8,0},{9,17... | collective-permute-start | bytes 1622024 | tf_op jit(solution)/shard_map/ppermute | solution.py:52
  46.8 15.3 %collective-permute-start.12 = (bf16[2,528,256]{2,1,0:T(8,128)(2,1)S(1)}, bf16[2,528,256]{2,1,0:T(8,128)(2,1)S(1)}, u32[]{:S(2)}, u32[]{:S(2)}) collective-permute-start(bf16[2,528,256]{2,1,0:T(8,128)(2,1)S(1)} %shard_map.132), channel_id=1, source_target_pairs={{0,24},{1,9},{2,26},{3,11},{4,28},{5,13},{6,30},{7,15},{8,0},{9,17... | collective-permute-start | bytes 1622024 | tf_op jit(solution)/shard_map/ppermute | solution.py:52
  47.6 5.7 %copy-start.10 = (s32[1,512]{1,0:T(1,128)S(1)}, s32[1,512]{1,0:T(1,128)}, u32[]{:S(2)}) copy-start(s32[1,512]{1,0:T(1,128)} %i_ref.3) | copy-start | bytes 6148
  50.9 4.4 %collective-permute-start.16 = (bf16[512,512]{1,0:T(8,128)(2,1)S(1)}, bf16[512,512]{1,0:T(8,128)(2,1)S(1)}, u32[]{:S(2)}, u32[]{:S(2)}) collective-permute-start(bf16[512,512]{1,0:T(8,128)(2,1)S(1)} %bitcast.52), channel_id=1, source_target_pairs={{0,1},{1,0},{2,3},{3,2},{4,5},{5,4},{6,7},{7,6},{8,9},{9,8},{10,11... | collective-permute-start | bytes 1572872 | tf_op jit(solution)/shard_map/ppermute | solution.py:52
  53.3 2.0 %collective-permute-start.15 = (s32[1,512]{1,0:T(1,128)S(1)}, s32[1,512]{1,0:T(1,128)S(1)}, u32[]{:S(2)}, u32[]{:S(2)}) collective-permute-start(s32[1,512]{1,0:T(1,128)S(1)} %copy-done.10), channel_id=1, source_target_pairs={{0,1},{1,0},{2,3},{3,2},{4,5},{5,4},{6,7},{7,6},{8,9},{9,8},{10,11... | collective-permute-start | bytes 6152 | tf_op jit(solution)/shard_map/ppermute | solution.py:52
  62.1 6.6 %collective-permute-start.18 = (bf16[528,256]{1,0:T(8,128)(2,1)S(1)}, bf16[528,256]{1,0:T(8,128)(2,1)S(1)}, u32[]{:S(2)}, u32[]{:S(2)}) collective-permute-start(bf16[528,256]{1,0:T(8,128)(2,1)S(1)} %slice_bitcast_fusion.1), channel_id=1, source_target_pairs={{0,24},{1,9},{2,26},{3,11},{4,28},{5,13},{6,30},{7,15},{8,0},{9,17... | collective-permute-start | bytes 811016 | tf_op jit(solution)/shard_map/ppermute | solution.py:52
  68.8 3.2 %collective-permute-start.19 = (f32[8,256]{1,0:T(8,128)S(1)}, f32[8,256]{1,0:T(8,128)S(1)}, u32[]{:S(2)}, u32[]{:S(2)}) collective-permute-start(f32[8,256]{1,0:T(8,128)S(1)} %shard_map.137.n_ref), channel_id=1, source_target_pairs={{0,1},{1,0},{2,3},{3,2},{4,5},{5,4},{6,7},{7,6},{8,9},{9,8},{10,11... | collective-permute-start | bytes 24584 | tf_op jit(solution)/shard_map/ppermute | solution.py:52
  71.9 2.7 %collective-permute-start.20 = (bf16[512,1024]{1,0:T(8,128)(2,1)S(1)}, bf16[512,1024]{1,0:T(8,128)(2,1)S(1)}, u32[]{:S(2)}, u32[]{:S(2)}) collective-permute-start(bf16[512,1024]{1,0:T(8,128)(2,1)S(1)} %get-tuple-element.112), channel_id=1, source_target_pairs={{0,1},{1,0},{2,3},{3,2},{4,5},{5,4},{6,7},{7,6},{8,9},{9,8},{10,11... | collective-permute-start | bytes 3145736 | tf_op jit(solution)/shard_map/ppermute | solution.py:52
  75.2 6.8 %collective-permute-start.21 = (bf16[1,512,256]{2,1,0:T(8,128)(2,1)S(1)}, bf16[1,512,256]{2,1,0:T(8,128)(2,1)S(1)}, u32[]{:S(2)}, u32[]{:S(2)}) collective-permute-start(bf16[1,512,256]{2,1,0:T(8,128)(2,1)S(1)} %get-tuple-element.117), channel_id=1, source_target_pairs={{0,8},{1,25},{2,10},{3,27},{4,12},{5,29},{6,14},{7,31},{8,16},{9,1... | collective-permute-start | bytes 786440 | tf_op jit(solution)/shard_map/ppermute | solution.py:52
  80.2 8.4 %collective-permute-start.22 = (bf16[2,512,256]{2,1,0:T(8,128)(2,1)S(1)}, bf16[2,512,256]{2,1,0:T(8,128)(2,1)S(1)}, u32[]{:S(2)}, u32[]{:S(2)}) collective-permute-start(bf16[2,512,256]{2,1,0:T(8,128)(2,1)S(1)} %get-tuple-element.121), channel_id=1, source_target_pairs={{0,8},{1,25},{2,10},{3,27},{4,12},{5,29},{6,14},{7,31},{8,16},{9,1... | collective-permute-start | bytes 1572872 | tf_op jit(solution)/shard_map/ppermute | solution.py:52
  80.3 5.2 %collective-permute-start.23 = (f32[256,128]{1,0:T(8,128)S(1)}, f32[256,128]{1,0:T(8,128)S(1)}, u32[]{:S(2)}, u32[]{:S(2)}) collective-permute-start(f32[256,128]{1,0:T(8,128)S(1)} %add.400), channel_id=1, source_target_pairs={{0,32},{32,0},{64,96},{96,64},{128,160},{160,128},{192,224},{224,1... | collective-permute-start | bytes 393224 | tf_op jit(solution)/shard_map/ppermute | solution.py:452
  82.0 12.2 %collective-permute-start.25 = (bf16[2,512,256]{2,1,0:T(8,128)(2,1)S(1)}, bf16[2,512,256]{2,1,0:T(8,128)(2,1)S(1)}, u32[]{:S(2)}, u32[]{:S(2)}) collective-permute-start(bf16[2,512,256]{2,1,0:T(8,128)(2,1)S(1)} %shard_map.143), channel_id=1, source_target_pairs={{0,8},{1,25},{2,10},{3,27},{4,12},{5,29},{6,14},{7,31},{8,16},{9,1... | collective-permute-start | bytes 1572872 | tf_op jit(solution)/shard_map/ppermute | solution.py:52
  88.8 19.5 %collective-permute-start.24 = (bf16[4,512,256]{2,1,0:T(8,128)(2,1)S(1)}, bf16[4,512,256]{2,1,0:T(8,128)(2,1)S(1)}, u32[]{:S(2)}, u32[]{:S(2)}) collective-permute-start(bf16[4,512,256]{2,1,0:T(8,128)(2,1)S(1)} %shard_map.145), channel_id=1, source_target_pairs={{0,8},{1,25},{2,10},{3,27},{4,12},{5,29},{6,14},{7,31},{8,16},{9,1... | collective-permute-start | bytes 3145736 | tf_op jit(solution)/shard_map/ppermute | solution.py:52
  94.2 3.8 %collective-permute-start.26 = (bf16[2,512,256]{2,1,0:T(8,128)(2,1)S(1)}, bf16[2,512,256]{2,1,0:T(8,128)(2,1)S(1)}, u32[]{:S(2)}, u32[]{:S(2)}) collective-permute-start(bf16[2,512,256]{2,1,0:T(8,128)(2,1)S(1)} %collective-permute-done.25.refs_1_), channel_id=1, source_target_pairs={{0,1},{1,0},{2,3},{3,2},{4,5},{5,4},{6,7},{7,6},{8,9},{9,8},{10,11... | collective-permute-start | bytes 1572872 | tf_op jit(solution)/shard_map/ppermute | solution.py:52
  96.1 12.1 %collective-permute-start.28 = (bf16[1,512,256]{2,1,0:T(8,128)(2,1)S(1)}, bf16[1,512,256]{2,1,0:T(8,128)(2,1)S(1)}, u32[]{:S(2)}, u32[]{:S(2)}) collective-permute-start(bf16[1,512,256]{2,1,0:T(8,128)(2,1)S(1)} %get-tuple-element.128), channel_id=1, source_target_pairs={{0,8},{1,25},{2,10},{3,27},{4,12},{5,29},{6,14},{7,31},{8,16},{9,1... | collective-permute-start | bytes 786440 | tf_op jit(solution)/shard_map/ppermute | solution.py:52
  98.1 10.2 %collective-permute-start.27 = (bf16[1,512,256]{2,1,0:T(8,128)(2,1)S(1)}, bf16[1,512,256]{2,1,0:T(8,128)(2,1)S(1)}, u32[]{:S(2)}, u32[]{:S(2)}) collective-permute-start(bf16[1,512,256]{2,1,0:T(8,128)(2,1)S(1)} %shard_map.147), channel_id=1, source_target_pairs={{0,2},{1,7},{2,4},{3,1},{4,6},{5,3},{6,0},{7,5},{8,10},{9,15},{10,... | collective-permute-start | bytes 786440 | tf_op jit(solution)/shard_map/ppermute | solution.py:52
  108.3 2.9 %collective-permute-start.29 = (bf16[4,512,256]{2,1,0:T(8,128)(2,1)S(1)}, bf16[4,512,256]{2,1,0:T(8,128)(2,1)S(1)}, u32[]{:S(2)}, u32[]{:S(2)}) collective-permute-start(bf16[4,512,256]{2,1,0:T(8,128)(2,1)S(1)} %collective-permute-done.24.refs_1_), channel_id=1, source_target_pairs={{0,1},{1,0},{2,3},{3,2},{4,5},{5,4},{6,7},{7,6},{8,9},{9,8},{10,11... | collective-permute-start | bytes 3145736 | tf_op jit(solution)/shard_map/ppermute | solution.py:52
  111.4 11.2 %copy-start.5 = (f32[256,512]{1,0:T(8,128)S(1)}, f32[256,512]{1,0:T(8,128)}, u32[]{:S(2)}) copy-start(f32[256,512]{1,0:T(8,128)} %m_ref.1) | copy-start | bytes 1572868
  111.5 12.3 %collective-permute-start.30 = (bf16[2,512,256]{2,1,0:T(8,128)(2,1)S(1)}, bf16[2,512,256]{2,1,0:T(8,128)(2,1)S(1)}, u32[]{:S(2)}, u32[]{:S(2)}) collective-permute-start(bf16[2,512,256]{2,1,0:T(8,128)(2,1)S(1)} %shard_map.149), channel_id=1, source_target_pairs={{0,8},{1,25},{2,10},{3,27},{4,12},{5,29},{6,14},{7,31},{8,16},{9,1... | collective-permute-start | bytes 1572872 | tf_op jit(solution)/shard_map/ppermute | solution.py:52
  113.4 14.6 %collective-permute-start.31 = (bf16[2,512,256]{2,1,0:T(8,128)(2,1)S(1)}, bf16[2,512,256]{2,1,0:T(8,128)(2,1)S(1)}, u32[]{:S(2)}, u32[]{:S(2)}) collective-permute-start(bf16[2,512,256]{2,1,0:T(8,128)(2,1)S(1)} %shard_map.148), channel_id=1, source_target_pairs={{0,2},{1,7},{2,4},{3,1},{4,6},{5,3},{6,0},{7,5},{8,10},{9,15},{10,... | collective-permute-start | bytes 1572872 | tf_op jit(solution)/shard_map/ppermute | solution.py:52
  117.0 5.6 %collective-permute-start.32 = (f32[256,128]{1,0:T(8,128)S(1)}, f32[256,128]{1,0:T(8,128)S(1)}, u32[]{:S(2)}, u32[]{:S(2)}) collective-permute-start(f32[256,128]{1,0:T(8,128)S(1)} %add.401), channel_id=1, source_target_pairs={{0,64},{32,96},{64,0},{96,32},{128,192},{160,224},{192,128},{224,1... | collective-permute-start | bytes 393224 | tf_op jit(solution)/shard_map/ppermute | solution.py:452
  122.6 8.0 %copy-start.6 = (f32[1,256,512]{2,1,0:T(8,128)S(1)}, f32[1,256,512]{2,1,0:T(8,128)}, u32[]{:S(2)}) copy-start(f32[1,256,512]{2,1,0:T(8,128)} %param.13) | copy-start | bytes 1572868
  122.6 8.0 %copy-start.7 = (f32[1,256,512]{2,1,0:T(8,128)S(1)}, f32[1,256,512]{2,1,0:T(8,128)}, u32[]{:S(2)}) copy-start(f32[1,256,512]{2,1,0:T(8,128)} %param.14) | copy-start | bytes 1572868
  123.8 6.8 %copy-start.8 = (f32[256,512]{1,0:T(8,128)S(1)}, f32[256,512]{1,0:T(8,128)}, u32[]{:S(2)}) copy-start(f32[256,512]{1,0:T(8,128)} %get-tuple-element.72.o_ref) | copy-start | bytes 1572868
  128.0 1.9 %collective-permute-start.33 = (bf16[2,512,256]{2,1,0:T(8,128)(2,1)S(1)}, bf16[2,512,256]{2,1,0:T(8,128)(2,1)S(1)}, u32[]{:S(2)}, u32[]{:S(2)}) collective-permute-start(bf16[2,512,256]{2,1,0:T(8,128)(2,1)S(1)} %collective-permute-done.30.refs_1_), channel_id=1, source_target_pairs={{0,1},{1,0},{2,3},{3,2},{4,5},{5,4},{6,7},{7,6},{8,9},{9,8},{10,11... | collective-permute-start | bytes 1572872 | tf_op jit(solution)/shard_map/ppermute | solution.py:52
  128.0 2.7 %collective-permute-start.34 = (bf16[2,512,256]{2,1,0:T(8,128)(2,1)S(1)}, bf16[2,512,256]{2,1,0:T(8,128)(2,1)S(1)}, u32[]{:S(2)}, u32[]{:S(2)}) collective-permute-start(bf16[2,512,256]{2,1,0:T(8,128)(2,1)S(1)} %collective-permute-done.31.p1), channel_id=1, source_target_pairs={{0,1},{1,0},{2,3},{3,2},{4,5},{5,4},{6,7},{7,6},{8,9},{9,8},{10,11... | collective-permute-start | bytes 1572872 | tf_op jit(solution)/shard_map/ppermute | solution.py:52
